TPU v7x, 32 devices: a whole 2x2x4 slice. The times are simulated.
32 devices in a mesh: dp: 8 (over z, y), tensor: 4 (over x, core).
Axes of the slice: x: 2, y: 2, z: 4, core: 2. Of those that a mesh axis runs over, the one named last changes fastest.
Arguments:
- tokens: bfloat16 [12288, 1024], P(('dp', 'tensor')), may hold values from -6 to 6
- encoder: bfloat16 [8, 1024, 1024], P('dp', 'tensor'), may hold values from -6 to 6
- seg_ids: int32 [8, 1536], P('dp'), may hold values from 0 to 3, as said below
- enc_lens: int32 [8], P('dp'), may hold values from 128 to 1024, as said below
- attn_qkv: float32 [3, 1024, 1024], P(None, 'dp', 'tensor'), may hold values from -0.1875 to 0.1875
- attn_out: float32 [1024, 1024], P('tensor', 'dp'), may hold values from -0.5 to 0.5
- cross_q: float32 [1024, 1024], P('dp', 'tensor'), may hold values from -0.1875 to 0.1875
- cross_kv: float32 [2, 1024, 1024], P(None, 'dp', 'tensor'), may hold values from -0.1875 to 0.1875
- cross_out: float32 [1024, 1024], P('tensor', 'dp'), may hold values from -0.75 to 0.75
- ffn_in: float32 [1024, 4096], P('dp', 'tensor'), may hold values from -0.1875 to 0.1875
- ffn_out: float32 [4096, 1024], P('tensor', 'dp'), may hold values from -0.09375 to 0.09375
- norm_gains: float32 [3, 1024], replicated, may hold values from 0.5 to 1.5
- norm_biases: float32 [3, 1024], replicated, may hold values from -1.5 to 1.5
- out_grad: bfloat16 [12288, 1024], P(('dp', 'tensor')), may hold values from -6 to 6
Outputs:
- out_tokens: bfloat16 [12288, 1024], P(('dp', 'tensor'))
- in_grad: float32 [12288, 1024], P(('dp', 'tensor'))
- enc_grad: float32 [8, 1024, 1024], P('dp', 'tensor')
- attn_qkv_grad: float32 [3, 1024, 1024], P(None, 'dp', 'tensor')
- attn_out_grad: float32 [1024, 1024], P('tensor', 'dp')
- cross_q_grad: float32 [1024, 1024], P('dp', 'tensor')
- cross_kv_grad: float32 [2, 1024, 1024], P(None, 'dp', 'tensor')
- cross_out_grad: float32 [1024, 1024], P('tensor', 'dp')
- ffn_in_grad: float32 [1024, 4096], P('dp', 'tensor')
- ffn_out_grad: float32 [4096, 1024], P('tensor', 'dp')
- gain_grad: float32 [3, 1024], replicated
- bias_grad: float32 [3, 1024], replicated
Inputs may be any that keep to these rules, and one draw needn't show every extreme that they name: `seg_ids`: in each sequence the document numbers never fall and every number 0 to 3 occurs; a document has 153 to 768 tokens, and one of each sequence has exactly 768. `enc_lens`: some sequence has all 1024 positions valid.
All inputs are finite; a program needn't handle non-finite values.
Results may differ from a plain program's by a relative error of at most 0.019.
Values may be sent and summed in bfloat16 or wider, within the bound.
A program may use at most 128 MiB of HBM per device.

v0:
```python
import jax
import jax.numpy as jnp
from jax import lax
from jax.sharding import PartitionSpec as P

HD = 64


epsilon = 1e-05
masked_score = -1e30


def matmul(left, right):
    return jnp.dot(left, right, preferred_element_type=jnp.float32)


def inner_rows(left, right):
    return lax.dot_general(
        left, right, (((0,), (0,)), ((), ())), preferred_element_type=jnp.float32
    )


def outer_cols(left, right):
    return lax.dot_general(
        left, right, (((1,), (1,)), ((), ())), preferred_element_type=jnp.float32
    )


def norm_forward(values_in, gain_row, bias_row):
    average = jnp.mean(values_in, axis=-1, keepdims=True)
    centred = values_in - average
    inverse = lax.rsqrt(jnp.mean(centred * centred, axis=-1, keepdims=True) + epsilon)
    unit_rows = centred * inverse
    return (unit_rows * gain_row + bias_row, unit_rows, inverse)


def norm_backward(incoming, unit_rows, inverse, gain_row):
    scaled = incoming * gain_row
    first_mean = jnp.mean(scaled, axis=-1, keepdims=True)
    second_mean = jnp.mean(scaled * unit_rows, axis=-1, keepdims=True)
    result = inverse * (scaled - first_mean - unit_rows * second_mean)
    return (result, jnp.sum(incoming * unit_rows, axis=0), jnp.sum(incoming, axis=0))


def attend(queries, key_rows, value_rows, allowed, score_scale):
    seq_len = queries.shape[0]
    block_rows = min(512, seq_len)

    def one_block(unused, block_index):
        row_start = block_index * block_rows
        query_block = lax.dynamic_slice_in_dim(queries, row_start, block_rows, 0)
        scores = (
            jnp.einsum("qhd,khd->hqk", query_block, key_rows, preferred_element_type=jnp.float32)
            * score_scale
        )
        scores = jnp.where(allowed(row_start, block_rows)[None], scores, masked_score)
        row_peak = jnp.max(scores, axis=-1, keepdims=True)
        exponent = jnp.exp(scores - row_peak)
        row_total = jnp.sum(exponent, axis=-1, keepdims=True)
        soft_probs = (exponent / row_total).astype(jnp.bfloat16)
        context = jnp.einsum(
            "hqk,khd->qhd", soft_probs, value_rows, preferred_element_type=jnp.float32
        )
        return (
            unused,
            (context.astype(jnp.bfloat16), row_peak[..., 0] + jnp.log(row_total[..., 0])),
        )

    indices = jnp.arange(seq_len // block_rows, dtype=jnp.int32)
    unused_out, (context, log_total) = lax.scan(one_block, None, indices)
    return (context.reshape(seq_len, -1), log_total)


def attend_back(queries, key_rows, value_rows, log_total, grad_context, allowed, score_scale):
    seq_len = queries.shape[0]
    block_rows = min(512, seq_len)

    def one_block(running, block_index):
        key_total, value_total = running
        row_start = block_index * block_rows
        query_block = lax.dynamic_slice_in_dim(queries, row_start, block_rows, 0)
        grad_block = lax.dynamic_slice_in_dim(grad_context, row_start, block_rows, 0)
        scores = (
            jnp.einsum("qhd,khd->hqk", query_block, key_rows, preferred_element_type=jnp.float32)
            * score_scale
        )
        scores = jnp.where(allowed(row_start, block_rows)[None], scores, masked_score)
        soft_probs = jnp.exp(scores - log_total[block_index][..., None])
        grad_probs = jnp.einsum(
            "qhd,khd->hqk", grad_block, value_rows, preferred_element_type=jnp.float32
        )
        inner_sum = jnp.sum(soft_probs * grad_probs, axis=-1, keepdims=True)
        grad_scores = (score_scale * soft_probs * (grad_probs - inner_sum)).astype(jnp.bfloat16)
        grad_query = jnp.einsum(
            "hqk,khd->qhd", grad_scores, key_rows, preferred_element_type=jnp.float32
        )
        key_total = key_total + jnp.einsum(
            "hqk,qhd->khd", grad_scores, query_block, preferred_element_type=jnp.float32
        )
        value_total = value_total + jnp.einsum(
            "hqk,qhd->khd",
            soft_probs.astype(jnp.bfloat16),
            grad_block,
            preferred_element_type=jnp.float32,
        )
        return ((key_total, value_total), grad_query.astype(jnp.bfloat16))

    start_totals = (
        jnp.zeros(key_rows.shape, jnp.float32),
        jnp.zeros(value_rows.shape, jnp.float32),
    )
    indices = jnp.arange(seq_len // block_rows, dtype=jnp.int32)
    (key_total, value_total), grad_query = lax.scan(one_block, start_totals, indices)
    key_count = key_rows.shape[0]
    return (
        grad_query.reshape(seq_len, -1),
        key_total.astype(jnp.bfloat16).reshape(key_count, -1),
        value_total.astype(jnp.bfloat16).reshape(key_count, -1),
    )


def on_device(
    tokens,
    encoder,
    seg_ids,
    enc_lens,
    attn_qkv,
    attn_out,
    cross_q,
    cross_kv,
    cross_out,
    ffn_in,
    ffn_out,
    norm_gains,
    norm_biases,
    out_grad,
):
    low_type = jnp.bfloat16
    self_proj, self_back, cross_query, cross_pair, cross_back, ffn_up, ffn_down = (
        lax.all_gather(attn_qkv.astype(low_type), "dp", axis=1, tiled=True),
        lax.all_gather(attn_out.astype(low_type), "dp", axis=1, tiled=True),
        lax.all_gather(cross_q.astype(low_type), "dp", axis=0, tiled=True),
        lax.all_gather(cross_kv.astype(low_type), "dp", axis=1, tiled=True),
        lax.all_gather(cross_out.astype(low_type), "dp", axis=1, tiled=True),
        lax.all_gather(ffn_in.astype(low_type), "dp", axis=0, tiled=True),
        lax.all_gather(ffn_out.astype(low_type), "dp", axis=1, tiled=True),
    )
    local_rows = tokens.shape[0]
    score_scale = HD ** (-0.5)
    segment = seg_ids[0]
    enc_length = enc_lens[0]
    seq_len = segment.shape[0]
    heads_here = self_back.shape[0] // HD
    positions = jnp.arange(seq_len, dtype=jnp.int32)

    def self_allowed(row_start, block_rows):
        row_ids = row_start + jnp.arange(block_rows, dtype=jnp.int32)
        row_segments = lax.dynamic_slice_in_dim(segment, row_start, block_rows, 0)
        return (row_segments[:, None] == segment[None, :]) & (
            row_ids[:, None] >= positions[None, :]
        )

    enc_full = lax.all_gather(encoder, "tensor", axis=1, tiled=True)[0]
    enc_count = enc_full.shape[0]
    enc_positions = jnp.arange(enc_count, dtype=jnp.int32)

    def cross_allowed(row_start, block_rows):
        return jnp.broadcast_to(enc_positions[None, :] < enc_length, (block_rows, enc_count))

    def gather_rows(values_low):
        return lax.all_gather(values_low, "tensor", axis=0, tiled=True)

    def gather_grads(values_low):
        return lax.all_gather(values_low, "tensor", axis=0, tiled=True)

    def branch_sum(make_term):
        return lax.psum_scatter(
            make_term(jnp.int32(0), local_rows * lax.axis_size("tensor")),
            "tensor",
            scatter_dimension=0,
            tiled=True,
        )

    def input_sum(make_term):
        return lax.psum_scatter(
            make_term(jnp.int32(0), lax.axis_size("tensor") * local_rows).astype(jnp.bfloat16),
            "tensor",
            scatter_dimension=0,
            tiled=True,
        ).astype(jnp.float32)

    head_shape = (seq_len, heads_here, HD)
    enc_shape = (enc_count, heads_here, HD)
    residual = tokens.astype(jnp.float32)
    normed, unit_one, inverse_one = norm_forward(residual, norm_gains[0], norm_biases[0])
    rows_one = gather_rows(normed.astype(low_type))
    projected = jnp.einsum(
        "sd,ide->ise", rows_one, self_proj, preferred_element_type=jnp.float32
    ).astype(low_type)
    queries_one = projected[0].reshape(head_shape)
    keys_one = projected[1].reshape(head_shape)
    values_one = projected[2].reshape(head_shape)
    context_one, total_one = attend(queries_one, keys_one, values_one, self_allowed, score_scale)

    def self_term(row_start, row_count):
        return matmul(context_one, self_back)

    residual_one = residual + branch_sum(self_term)
    normed, unit_two, inverse_two = norm_forward(residual_one, norm_gains[1], norm_biases[1])
    rows_two = gather_rows(normed.astype(low_type))
    queries_two = matmul(rows_two, cross_query).astype(low_type).reshape(head_shape)
    enc_pair = jnp.einsum(
        "sd,ide->ise", enc_full, cross_pair, preferred_element_type=jnp.float32
    ).astype(low_type)
    keys_two = enc_pair[0].reshape(enc_shape)
    values_two = enc_pair[1].reshape(enc_shape)
    context_two, total_two = attend(queries_two, keys_two, values_two, cross_allowed, score_scale)

    def cross_term(row_start, row_count):
        return matmul(context_two, cross_back)

    residual_two = residual_one + branch_sum(cross_term)
    normed, unit_three, inverse_three = norm_forward(residual_two, norm_gains[2], norm_biases[2])
    rows_three = gather_rows(normed.astype(low_type))
    inner_pre = matmul(rows_three, ffn_up)
    active = jax.nn.silu(inner_pre).astype(low_type)

    def ffn_term(row_start, row_count):
        return matmul(active, ffn_down)

    out_tokens = (residual_two + branch_sum(ffn_term)).astype(low_type)
    self_proj, self_back, cross_query, cross_pair, cross_back, ffn_up, ffn_down = (
        lax.all_gather(attn_qkv.astype(low_type), "dp", axis=1, tiled=True),
        lax.all_gather(attn_out.astype(low_type), "dp", axis=1, tiled=True),
        lax.all_gather(cross_q.astype(low_type), "dp", axis=0, tiled=True),
        lax.all_gather(cross_kv.astype(low_type), "dp", axis=1, tiled=True),
        lax.all_gather(cross_out.astype(low_type), "dp", axis=1, tiled=True),
        lax.all_gather(ffn_in.astype(low_type), "dp", axis=0, tiled=True),
        lax.all_gather(ffn_out.astype(low_type), "dp", axis=1, tiled=True),
    )
    grad_total = out_grad.astype(jnp.float32)
    grads_three = gather_grads(out_grad)
    grad_active = outer_cols(grads_three, ffn_down)
    sigmoid_pre = jax.nn.sigmoid(inner_pre)
    slope = sigmoid_pre * (1.0 + inner_pre * (1.0 - sigmoid_pre))
    grad_inner = (grad_active * slope).astype(low_type)
    down_grad = inner_rows(active, grads_three)
    up_grad = inner_rows(rows_three, grad_inner)

    def ffn_back_term(row_start, row_count):
        return outer_cols(grad_inner, ffn_up)

    grad_normed = input_sum(ffn_back_term)
    grad_residual, gain_three, bias_three = norm_backward(
        grad_normed, unit_three, inverse_three, norm_gains[2]
    )
    grad_total = grad_total + grad_residual
    grads_two = gather_grads(grad_total.astype(low_type))
    grad_context = outer_cols(grads_two, cross_back).astype(low_type)
    cross_back_grad = inner_rows(context_two, grads_two)
    grad_queries, grad_keys, grad_values = attend_back(
        queries_two,
        keys_two,
        values_two,
        total_two,
        grad_context.reshape(head_shape),
        cross_allowed,
        score_scale,
    )
    cross_query_grad = inner_rows(rows_two, grad_queries)
    cross_pair_grad = jnp.stack(
        [inner_rows(enc_full, grad_keys), inner_rows(enc_full, grad_values)]
    )

    def query_back_term(row_start, row_count):
        return outer_cols(grad_queries, cross_query)

    grad_normed = input_sum(query_back_term)
    key_part = grad_keys
    value_part = grad_values
    enc_grad = lax.psum_scatter(
        (outer_cols(key_part, cross_pair[0]) + outer_cols(value_part, cross_pair[1])).astype(
            jnp.bfloat16
        ),
        "tensor",
        scatter_dimension=0,
        tiled=True,
    ).astype(jnp.float32)[None]
    grad_residual, gain_two, bias_two = norm_backward(
        grad_normed, unit_two, inverse_two, norm_gains[1]
    )
    grad_total = grad_total + grad_residual
    grads_one = gather_grads(grad_total.astype(low_type))
    grad_context = outer_cols(grads_one, self_back).astype(low_type)
    self_back_grad = inner_rows(context_one, grads_one)
    grad_queries, grad_keys, grad_values = attend_back(
        queries_one,
        keys_one,
        values_one,
        total_one,
        grad_context.reshape(head_shape),
        self_allowed,
        score_scale,
    )
    grad_proj = jnp.stack([grad_queries, grad_keys, grad_values])
    self_proj_grad = jnp.einsum(
        "sd,ise->ide", rows_one, grad_proj, preferred_element_type=jnp.float32
    )

    def proj_back_term(row_start, row_count):
        return jnp.einsum("ise,ide->sd", grad_proj, self_proj, preferred_element_type=jnp.float32)

    grad_normed = input_sum(proj_back_term)
    grad_residual, gain_one, bias_one = norm_backward(
        grad_normed, unit_one, inverse_one, norm_gains[0]
    )
    in_grad = grad_total + grad_residual
    (
        self_proj_grad,
        self_back_grad,
        cross_query_grad,
        cross_pair_grad,
        cross_back_grad,
        up_grad,
        down_grad,
    ) = (
        lax.psum_scatter(self_proj_grad, "dp", scatter_dimension=1, tiled=True),
        lax.psum_scatter(self_back_grad, "dp", scatter_dimension=1, tiled=True),
        lax.psum_scatter(cross_query_grad, "dp", scatter_dimension=0, tiled=True),
        lax.psum_scatter(cross_pair_grad, "dp", scatter_dimension=1, tiled=True),
        lax.psum_scatter(cross_back_grad, "dp", scatter_dimension=1, tiled=True),
        lax.psum_scatter(up_grad, "dp", scatter_dimension=0, tiled=True),
        lax.psum_scatter(down_grad, "dp", scatter_dimension=1, tiled=True),
    )
    gain_grad, bias_grad = lax.psum(
        (jnp.stack([gain_one, gain_two, gain_three]), jnp.stack([bias_one, bias_two, bias_three])),
        ("dp", "tensor"),
    )
    return (
        out_tokens,
        in_grad,
        enc_grad,
        self_proj_grad,
        self_back_grad,
        cross_query_grad,
        cross_pair_grad,
        cross_back_grad,
        up_grad,
        down_grad,
        gain_grad,
        bias_grad,
    )


def solution(mesh):
    in_specs = (
        P(("dp", "tensor"), None),
        P("dp", "tensor", None),
        P("dp", None),
        P("dp"),
        P(None, "dp", "tensor"),
        P("tensor", "dp"),
        P("dp", "tensor"),
        P(None, "dp", "tensor"),
        P("tensor", "dp"),
        P("dp", "tensor"),
        P("tensor", "dp"),
        P(),
        P(),
        P(("dp", "tensor"), None),
    )
    out_specs = (
        P(("dp", "tensor"), None),
        P(("dp", "tensor"), None),
        P("dp", "tensor", None),
        P(None, "dp", "tensor"),
        P("tensor", "dp"),
        P("dp", "tensor"),
        P(None, "dp", "tensor"),
        P("tensor", "dp"),
        P("dp", "tensor"),
        P("tensor", "dp"),
        P(),
        P(),
    )
    return jax.shard_map(
        on_device, mesh=mesh, in_specs=in_specs, out_specs=out_specs, check_vma=False
    )
```

profile of v0, /device:TPU:0, one launch (start us, length us, event | category | flops | bytes accessed | tf_op | source)
XLA Modules:
  0.0 1455.7 jit_solution(15388323043238652915)
XLA Ops:
  17.4 33.5 %all_gather.51 = bf16[256,1024]{1,0:T(8,128)(2,1)} all-gather(bf16[256,128]{1,0:T(8,128)(2,1)S(1)} %convert_element_type.160), channel_id=1, replica_groups=mesh['dp'=8,'tensor'=4] {'dp'}, dimensions={1}, use_global_device_ids=true | all-gather | bytes 589824 | tf_op jit(solution)/shard_map/all_gather | solution.py:141
  50.9 11.9 all-gather.14.cloned.1.call-done
  62.8 29.3 %all-gather.12.cloned.1.call-done = bf16[1536,1024]{1,0:T(8,128)(2,1)} async-done(((bf16[384,1024]{1,0:T(8,128)(2,1)}), bf16[1536,1024]{1,0:T(8,128)(2,1)}) %all-gather.12.cloned.1.call-update) | async-done | bytes 3145744 | tf_op jit(solution)/shard_map/all_gather | solution.py:171
  97.4 38.7 %while.56 = (s32[]{:T(128)}, bf16[3,512,4,64]{1,3,2,0:T(8,128)(2,1)S(1)}, f32[3,4,512]{2,1,0:T(4,128)S(1)}, s32[3]{0:T(128)S(1)}, s32[1536]{0:T(1024)S(1)}, /*in...) while((s32[]{:T(128)}, ...), condition=%wide.region_5.6_spmd.clone, body=%wide.region_2.5_spmd.clone.sunk | while | flops 845543936 | bytes 43086036 | solution.py:70
  144.2 56.0 %reduce-scatter.15.cloned.1.call-done = f32[384,1024]{1,0:T(8,128)} async-done(((f32[1536,1024]{1,0:T(8,128)}), f32[384,1024]{1,0:T(8,128)}) %reduce-scatter.15.cloned.1.call-update) | async-done | bytes 1572880 | tf_op jit(solution)/shard_map/reduce_scatter | solution.py:177
  203.5 29.3 %all_gather.56 = bf16[256,1024]{1,0:T(8,128)(2,1)} all-gather(bf16[256,128]{1,0:T(8,128)(2,1)S(1)} %convert_element_type.167), channel_id=1, replica_groups=mesh['dp'=8,'tensor'=4] {'dp'}, dimensions={1}, use_global_device_ids=true | all-gather | bytes 589824 | tf_op jit(solution)/shard_map/all_gather | solution.py:144
  232.8 33.4 %all_gather.53 = bf16[1024,256]{1,0:T(8,128)(2,1)} all-gather(bf16[128,256]{1,0:T(8,128)(2,1)S(1)} %convert_element_type.162), channel_id=1, replica_groups=mesh['dp'=8,'tensor'=4] {'dp'}, dimensions={0}, use_global_device_ids=true | all-gather | bytes 589824 | tf_op jit(solution)/shard_map/all_gather | solution.py:142
  273.7 27.3 %all-gather.16.cloned.1.call-done = bf16[1536,1024]{1,0:T(8,128)(2,1)} async-done(((bf16[384,1024]{1,0:T(8,128)(2,1)}), bf16[1536,1024]{1,0:T(8,128)(2,1)}) %all-gather.16.cloned.1.call-update) | async-done | bytes 3145744 | tf_op jit(solution)/shard_map/all_gather | solution.py:171
  305.1 25.5 %while.57 = (s32[]{:T(128)}, bf16[3,512,4,64]{1,3,2,0:T(8,128)(2,1)}, f32[3,4,512]{2,1,0:T(4,128)S(1)}, s32[]{:T(128)}, s32[3]{0:T(128)S(1)}, /*index=5*/bf16[15...) while((s32[]{:T(128)}, ...), condition=%wide.region_12.13_spmd.clone, body=%wide.region_9.12_spmd.clone.sunk | while | flops 562166784 | bytes 26808520 | solution.py:70
  339.2 56.6 %reduce-scatter.17.cloned.1.call-done = f32[384,1024]{1,0:T(8,128)} async-done(((f32[1536,1024]{1,0:T(8,128)}), f32[384,1024]{1,0:T(8,128)}) %reduce-scatter.17.cloned.1.call-update) | async-done | bytes 1572880 | tf_op jit(solution)/shard_map/reduce_scatter | solution.py:177
  401.8 46.0 %all-gather.24.cloned.1.call-done = bf16[1024,1024]{1,0:T(8,128)(2,1)} async-done(((bf16[128,1024]{1,0:T(8,128)(2,1)}), bf16[1024,1024]{1,0:T(8,128)(2,1)}) %all-gather.24.cloned.1.call-update) | async-done | bytes 2097168 | tf_op jit(solution)/shard_map/all_gather | solution.py:145
  447.8 29.2 %all-gather.22.cloned.1.call-done = bf16[1536,1024]{1,0:T(8,128)(2,1)} async-done(((bf16[384,1024]{1,0:T(8,128)(2,1)}), bf16[1536,1024]{1,0:T(8,128)(2,1)}) %all-gather.22.cloned.1.call-update) | async-done | bytes 3145744 | tf_op jit(solution)/shard_map/all_gather | solution.py:171
  477.0 10.3 multiply_convert_fusion.3
  487.2 43.3 %all-gather.26.cloned.1.call-done = bf16[1024,1024]{1,0:T(8,128)(2,1)} async-done(((bf16[1024,128]{1,0:T(8,128)(2,1)}), bf16[1024,1024]{1,0:T(8,128)(2,1)}) %all-gather.26.cloned.1.call-update) | async-done | bytes 2097168 | tf_op jit(solution)/shard_map/all_gather | solution.py:146
  530.5 28.3 %all-gather.28.cloned.1.call-done = bf16[1536,1024]{1,0:T(8,128)(2,1)} async-done(((bf16[384,1024]{1,0:T(8,128)(2,1)}), bf16[1536,1024]{1,0:T(8,128)(2,1)}) %all-gather.28.cloned.1.call-update) | async-done | bytes 3145744 | tf_op jit(solution)/shard_map/all_gather | solution.py:174
  558.9 9.3 multiply_convert_fusion.2
  574.8 8.9 fusion.150
  583.8 29.1 %reduce-scatter.21.cloned.1.call-done = bf16[384,1024]{1,0:T(8,128)(2,1)} async-done(((bf16[1536,1024]{1,0:T(8,128)(2,1)}), bf16[384,1024]{1,0:T(8,128)(2,1)}) %reduce-scatter.21.cloned.1.call-update) | async-done | bytes 786448 | tf_op jit(solution)/shard_map/reduce_scatter | solution.py:185
  615.3 58.6 %reduce-scatter.19.cloned.1.call-done = f32[384,1024]{1,0:T(8,128)} async-done(((f32[1536,1024]{1,0:T(8,128)}), f32[384,1024]{1,0:T(8,128)}) %reduce-scatter.19.cloned.1.call-update) | async-done | bytes 1572880 | tf_op jit(solution)/shard_map/reduce_scatter | solution.py:177
  678.5 28.4 %all-gather.30.cloned.1.call-done = bf16[1536,1024]{1,0:T(8,128)(2,1)} async-done(((bf16[384,1024]{1,0:T(8,128)(2,1)}), bf16[1536,1024]{1,0:T(8,128)(2,1)}) %all-gather.30.cloned.1.call-update) | async-done | bytes 3145744 | tf_op jit(solution)/shard_map/all_gather | solution.py:174
  711.9 47.2 %while.58 = (s32[]{:T(128)}, f32[1024,4,64]{0,2,1:T(8,128)S(1)}, f32[1024,4,64]{0,2,1:T(8,128)}, bf16[3,512,4,64]{1,3,2,0:T(8,128)(2,1)}, s32[3]{0:T(128)S(1)}, ...) while((s32[]{:T(128)}, f32[1024,4,64]{0,2,1:T(8,128)S(1)}, ...), condition=%wide.region_22.23_spmd.clone, body=%wide.region_20.22_spmd.clone.sunk | while | flops 1376910336 | bytes 81588600 | solution.py:113
  765.4 37.7 %reduce-scatter.23.cloned.1.call-done = bf16[384,1024]{1,0:T(8,128)(2,1)} async-done(((bf16[1536,1024]{1,0:T(8,128)(2,1)}), bf16[384,1024]{1,0:T(8,128)(2,1)}) %reduce-scatter.23.cloned.1.call-update) | async-done | bytes 786448 | tf_op jit(solution)/shard_map/reduce_scatter | solution.py:185
  818.1 19.5 %all-gather.32.cloned.1.call-done = bf16[1536,1024]{1,0:T(8,128)(2,1)} async-done(((bf16[384,1024]{1,0:T(8,128)(2,1)}), bf16[1536,1024]{1,0:T(8,128)(2,1)}) %all-gather.32.cloned.1.call-update) | async-done | bytes 3145744 | tf_op jit(solution)/shard_map/all_gather | solution.py:174
  842.4 84.4 %while.59 = (s32[]{:T(128)}, f32[1536,4,64]{0,2,1:T(8,128)}, f32[1536,4,64]{0,2,1:T(8,128)}, bf16[3,512,4,64]{1,3,2,0:T(8,128)(2,1)}, s32[3]{0:T(128)S(1)}, /*in...) while((s32[]{:T(128)}, f32[1536,4,64]{0,2,1:T(8,128)}, ...), condition=%wide.region_28.29_spmd.clone, body=%wide.region_26.28_spmd.clone.sunk | while | flops 2048784896 | bytes 134287744 | solution.py:113
  981.1 40.6 %reduce-scatter.29.cloned.1.call-done = f32[3,128,256]{1,2,0:T(8,128)} async-done(((f32[3,1024,256]{1,2,0:T(8,128)}), f32[3,128,256]{1,2,0:T(8,128)}) %reduce-scatter.29.cloned.1.call-update) | async-done | bytes 393232 | tf_op jit(solution)/shard_map/reduce_scatter | solution.py:327
  1023.5 37.6 %reduce-scatter.25.cloned.1.call-done = bf16[384,1024]{1,0:T(8,128)(2,1)} async-done(((bf16[1536,1024]{1,0:T(8,128)(2,1)}), bf16[384,1024]{1,0:T(8,128)(2,1)}) %reduce-scatter.25.cloned.1.call-update) | async-done | bytes 786448 | tf_op jit(solution)/shard_map/reduce_scatter | solution.py:185
  1063.2 42.7 %all-reduce = (f32[3,1024]{1,0:T(4,128)}, f32[3,1024]{1,0:T(4,128)}) all-reduce(f32[3,1024]{1,0:T(4,128)S(1)} %pad_maximum_fusion.4, f32[3,1024]{1,0:T(4,128)S(1)} %pad_maximum_fusion.5), channel_id=1, replica_groups=mesh['dp'=8,'tensor'=4] {'dp','tensor'}, use_global_device_ids=true, to_apply=%region_43.44 | all-reduce | flops 6144 | bytes 49152 | tf_op jit(solution)/shard_map/psum | solution.py:335
  1108.7 46.7 %reduce-scatter.41.cloned.1.call-done = f32[1024,128]{1,0:T(8,128)} async-done(((f32[1024,1024]{1,0:T(8,128)}), f32[1024,128]{1,0:T(8,128)}) %reduce-scatter.41.cloned.1.call-update) | async-done | bytes 524304 | tf_op jit(solution)/shard_map/reduce_scatter | solution.py:333
  1155.4 91.9 %reduce-scatter.39.cloned.1.call-done = f32[128,1024]{1,0:T(8,128)} async-done(((f32[1024,1024]{1,0:T(8,128)}), f32[128,1024]{1,0:T(8,128)}) %reduce-scatter.39.cloned.1.call-update) | async-done | bytes 524304 | tf_op jit(solution)/shard_map/reduce_scatter | solution.py:332
  1247.3 68.1 %reduce-scatter.37.cloned.1.call-done = f32[256,128]{1,0:T(8,128)} async-done(((f32[256,1024]{1,0:T(8,128)}), f32[256,128]{1,0:T(8,128)}) %reduce-scatter.37.cloned.1.call-update) | async-done | bytes 131088 | tf_op jit(solution)/shard_map/reduce_scatter | solution.py:331
  1315.4 66.3 %reduce-scatter.33.cloned.1.call-done = f32[128,256]{1,0:T(8,128)} async-done(((f32[1024,256]{1,0:T(8,128)}), f32[128,256]{1,0:T(8,128)}) %reduce-scatter.33.cloned.1.call-update) | async-done | bytes 131088 | tf_op jit(solution)/shard_map/reduce_scatter | solution.py:329
  1381.7 67.3 %reduce-scatter.31.cloned.1.call-done = f32[256,128]{1,0:T(8,128)} async-done(((f32[256,1024]{1,0:T(8,128)}), f32[256,128]{1,0:T(8,128)}) %reduce-scatter.31.cloned.1.call-update) | async-done | bytes 131088 | tf_op jit(solution)/shard_map/reduce_scatter | solution.py:328
  (396 shorter events, 333.4 us)
Async XLA Ops:
  7.2 55.6 %all-gather.14.cloned.1.call-start = ((), (), s32[]{:S(2)}) async-start(), calls=%async_computation.15 | async-start | bytes 1769472 | tf_op jit(solution)/shard_map/all_gather | solution.py:140
  9.1 83.0 %all-gather.12.cloned.1.call-start = ((), (), s32[]{:S(2)}) async-start(), calls=%async_computation.14 | async-start | bytes 3932160 | tf_op jit(solution)/shard_map/all_gather | solution.py:171
  10.5 86.6 %copy-start.44 = (f32[384]{0:T(512)}, f32[384]{0:T(512)S(1)}, u32[]{:S(2)}) copy-start(f32[384]{0:T(512)S(1)} %broadcast_multiply_fusion.8) | copy-start | bytes 4612
  13.4 188.8 %copy-start.42 = (f32[1,1024]{1,0:T(1,128)}, f32[1,1024]{1,0:T(1,128)S(1)}, u32[]{:S(2)}) copy-start(f32[1,1024]{1,0:T(1,128)S(1)} %get-tuple-element.515) | copy-start | bytes 12292
  17.2 182.9 %reduce-scatter.15.cloned.1.call-start = ((), (), s32[]{:S(2)}) async-start(), calls=%async_computation.16 | async-start | bytes 7864320 | tf_op jit(solution)/shard_map/reduce_scatter | solution.py:177
  141.7 124.5 %all-gather.18.cloned.1.call-start = ((), (), s32[]{:S(2)}) async-start(), calls=%async_computation.18 | async-start | bytes 1179648 | tf_op jit(solution)/shard_map/all_gather | solution.py:143
  143.3 127.1 %all-gather.20.cloned.1.call-start = ((), (), s32[]{:S(2)}) async-start(), calls=%async_computation.19 | async-start | bytes 2621440 | tf_op jit(solution)/shard_map/all_gather | solution.py:163
  143.9 157.2 %all-gather.16.cloned.1.call-start = ((), (), s32[]{:S(2)}) async-start(), calls=%async_computation.17 | async-start | bytes 3932160 | tf_op jit(solution)/shard_map/all_gather | solution.py:171
  201.8 193.9 %copy-start.6 = (f32[384,1024]{1,0:T(8,128)}, f32[384,1024]{1,0:T(8,128)S(1)}, u32[]{:S(2)}) copy-start(f32[384,1024]{1,0:T(8,128)S(1)} %get-tuple-element.498) | copy-start | bytes 4718596
  203.4 192.3 %reduce-scatter.17.cloned.1.call-start = ((), (), s32[]{:S(2)}) async-start(), calls=%async_computation.20 | async-start | bytes 7864320 | tf_op jit(solution)/shard_map/reduce_scatter | solution.py:177
  337.2 110.5 %all-gather.24.cloned.1.call-start = ((), (), s32[]{:S(2)}) async-start(), calls=%async_computation.22 | async-start | bytes 2359296 | tf_op jit(solution)/shard_map/all_gather | solution.py:145
  339.1 137.9 %all-gather.22.cloned.1.call-start = ((), (), s32[]{:S(2)}) async-start(), calls=%async_computation.21 | async-start | bytes 3932160 | tf_op jit(solution)/shard_map/all_gather | solution.py:171
  399.8 130.8 %all-gather.26.cloned.1.call-start = ((), (), s32[]{:S(2)}) async-start(), calls=%async_computation.23 | async-start | bytes 2359296 | tf_op jit(solution)/shard_map/all_gather | solution.py:146
  400.6 158.3 %all-gather.28.cloned.1.call-start = ((), (), s32[]{:S(2)}) async-start(), calls=%async_computation.25 | async-start | bytes 3932160 | tf_op jit(solution)/shard_map/all_gather | solution.py:174
  401.3 211.6 %reduce-scatter.21.cloned.1.call-start = ((), (), s32[]{:S(2)}) async-start(), calls=%async_computation.26 | async-start | bytes 3932160 | tf_op jit(solution)/shard_map/reduce_scatter | solution.py:185
  574.8 99.2 %reduce-scatter.19.cloned.1.call-start = ((), (), s32[]{:S(2)}) async-start(), calls=%async_computation.24 | async-start | bytes 7864320 | tf_op jit(solution)/shard_map/reduce_scatter | solution.py:177
  583.7 123.2 %all-gather.30.cloned.1.call-start = ((), (), s32[]{:S(2)}) async-start(), calls=%async_computation.27 | async-start | bytes 3932160 | tf_op jit(solution)/shard_map/all_gather | solution.py:174
  678.3 124.8 %reduce-scatter.23.cloned.1.call-start = ((), (), s32[]{:S(2)}) async-start(), calls=%async_computation.28 | async-start | bytes 3932160 | tf_op jit(solution)/shard_map/reduce_scatter | solution.py:185
  765.0 72.6 %all-gather.32.cloned.1.call-start = ((), (), s32[]{:S(2)}) async-start(), calls=%async_computation.29 | async-start | bytes 3932160 | tf_op jit(solution)/shard_map/all_gather | solution.py:174
  808.9 168.1 %reduce-scatter.35.cloned.1.call-start = ((), (), s32[]{:S(2)}) async-start(), calls=%async_computation.35 | async-start | bytes 2359296 | tf_op jit(solution)/shard_map/reduce_scatter | solution.py:330
  815.0 164.0 %reduce-scatter.27.cloned.1.call-start = ((), (), s32[]{:S(2)}) async-start(), calls=%async_computation.31 | async-start | bytes 2621440 | tf_op jit(solution)/shard_map/reduce_scatter | solution.py:281
  818.1 203.6 %reduce-scatter.29.cloned.1.call-start = ((), (), s32[]{:S(2)}) async-start(), calls=%async_computation.32 | async-start | bytes 3538944 | tf_op jit(solution)/shard_map/reduce_scatter | solution.py:327
  940.2 120.9 %reduce-scatter.25.cloned.1.call-start = ((), (), s32[]{:S(2)}) async-start(), calls=%async_computation.30 | async-start | bytes 3932160 | tf_op jit(solution)/shard_map/reduce_scatter | solution.py:185
  945.9 209.5 %reduce-scatter.41.cloned.1.call-start = ((), (), s32[]{:S(2)}) async-start(), calls=%async_computation.38 | async-start | bytes 4718592 | tf_op jit(solution)/shard_map/reduce_scatter | solution.py:333
  954.7 292.5 %reduce-scatter.39.cloned.1.call-start = ((), (), s32[]{:S(2)}) async-start(), calls=%async_computation.37 | async-start | bytes 4718592 | tf_op jit(solution)/shard_map/reduce_scatter | solution.py:332
  963.6 351.8 %reduce-scatter.37.cloned.1.call-start = ((), (), s32[]{:S(2)}) async-start(), calls=%async_computation.36 | async-start | bytes 1179648 | tf_op jit(solution)/shard_map/reduce_scatter | solution.py:331
  968.6 413.1 %reduce-scatter.33.cloned.1.call-start = ((), (), s32[]{:S(2)}) async-start(), calls=%async_computation.34 | async-start | bytes 1179648 | tf_op jit(solution)/shard_map/reduce_scatter | solution.py:329
  972.9 476.1 %reduce-scatter.31.cloned.1.call-start = ((), (), s32[]{:S(2)}) async-start(), calls=%async_computation.33 | async-start | bytes 1179648 | tf_op jit(solution)/shard_map/reduce_scatter | solution.py:328
  976.9 86.2 %copy-start.53 = (f32[1024]{0:T(1024)S(1)}, f32[1024]{0:T(1024)}, u32[]{:S(2)}) copy-start(f32[1024]{0:T(1024)} %get-tuple-element.399) | copy-start | bytes 12292
  976.9 86.2 %copy-start.52 = (f32[1024]{0:T(1024)S(1)}, f32[1024]{0:T(1024)}, u32[]{:S(2)}) copy-start(f32[1024]{0:T(1024)} %get-tuple-element.408) | copy-start | bytes 12292
  976.9 86.2 %copy-start.54 = (f32[1024]{0:T(1024)S(1)}, f32[1024]{0:T(1024)}, u32[]{:S(2)}) copy-start(f32[1024]{0:T(1024)} %get-tuple-element.407) | copy-start | bytes 12292
  976.9 128.9 %copy-start.16 = (f32[384,1024]{1,0:T(8,128)S(1)}, f32[384,1024]{1,0:T(8,128)}, u32[]{:S(2)}) copy-start(f32[384,1024]{1,0:T(8,128)} %get-tuple-element.492) | copy-start | bytes 4718596
  (64 other events, 1314.4 us)
Sparse Core Ops, SparseCore 0:
  10.7 52.0 all-gather.13
  64.9 27.1 all-gather.11
  141.8 58.3 reduce-scatter.14
  202.8 44.3 all-gather.17
  248.7 21.6 all-gather.19
  272.5 28.5 all-gather.15
  337.3 58.3 reduce-scatter.16
  398.4 49.3 all-gather.23
  449.9 27.0 all-gather.21
  479.4 51.0 all-gather.25
  532.1 26.7 all-gather.27
  574.9 37.9 reduce-scatter.20
  615.6 58.3 reduce-scatter.18
  678.4 28.5 all-gather.29
  765.1 37.9 reduce-scatter.22
  809.0 28.5 all-gather.31
  841.4 68.4 reduce-scatter.34
  912.4 30.4 reduce-scatter.26
  946.5 75.1 reduce-scatter.28
  1024.0 37.0 reduce-scatter.24
  1065.8 89.5 reduce-scatter.40
  1159.6 87.6 reduce-scatter.38
  1251.6 63.7 reduce-scatter.36
  1319.2 62.4 reduce-scatter.32
  1386.1 62.8 reduce-scatter.30
where the time goes:
time: 1470 us; the launch traced here: 1460 us
  waiting for transfers between devices  926 us (63%)
  matrix products  225 us (15%)
  blocking collectives  139 us (9%)
  other arithmetic  84.3 us (6%)
  local copies, waits for them, and re-layouts  44.8 us (3%)
  loops' own time  20.1 us (1%)
  between operations  15.1 us (1%)
    reduce_scatter x3, waiting for transfers between devices, branch_sum(): lax.psum_scatter(make_term(jnp.int32(0), local_rows * lax.axis_size('tens...  171 us
    reduce_scatter x3, waiting for transfers between devices, input_sum(): lax.psum_scatter(make_term(jnp.int32(0), lax.axis_size('tensor') * local_...  104 us
    reduce_scatter x1, waiting for transfers between devices, on_device(): lax.psum_scatter(up_grad, 'dp', scatter_dimension=0, tiled=True)  91.9 us
    all_gather x3, waiting for transfers between devices, gather_rows(): return lax.all_gather(values_low, 'tensor', axis=0, tiled=True)  85.9 us
    all_gather x3, waiting for transfers between devices, gather_grads(): return lax.all_gather(values_low, 'tensor', axis=0, tiled=True)  76.2 us
    reduce_scatter x1, waiting for transfers between devices, on_device(): lax.psum_scatter(cross_back_grad, 'dp', scatter_dimension=1, tiled=True)  68.1 us
    reduce_scatter x1, waiting for transfers between devices, on_device(): lax.psum_scatter(self_back_grad, 'dp', scatter_dimension=1, tiled=True)  67.3 us
    reduce_scatter x1, waiting for transfers between devices, on_device(): lax.psum_scatter(cross_query_grad, 'dp', scatter_dimension=0, tiled=True)  66.3 us
  transfers between devices with their start and end apart: 25, of which 22 were waited for; matrix products, arithmetic and copies ran while one was open for 13% of the time, Pallas kernels for 0%

commit v1 on v0

v1 whole, which is shorter than its diff:
```python
import functools

import jax
import jax.numpy as jnp
from jax import lax
from jax.experimental import pallas as pl
from jax.experimental.pallas import tpu as pltpu
from jax.sharding import Mesh
from jax.sharding import PartitionSpec as P

HD = 64
LANES = 128
PAIR = 2 * HD
RING = 4
epsilon = 1e-05
masked_score = -1e30
MESH = pl.DeviceIdType.MESH
low_type = jnp.bfloat16
f32 = jnp.float32
MIB = 1 << 20


def matmul(left, right):
    return jnp.dot(left, right, preferred_element_type=f32)


def inner_rows(left, right):
    return lax.dot_general(left, right, (((0,), (0,)), ((), ())), preferred_element_type=f32)


def outer_cols(left, right):
    return lax.dot_general(left, right, (((1,), (1,)), ((), ())), preferred_element_type=f32)


def norm_forward(values_in, gain_row, bias_row):
    average = jnp.mean(values_in, axis=-1, keepdims=True)
    centred = values_in - average
    inverse = lax.rsqrt(jnp.mean(centred * centred, axis=-1, keepdims=True) + epsilon)
    unit_rows = centred * inverse
    return (unit_rows * gain_row + bias_row, unit_rows, inverse)


def norm_backward(incoming, unit_rows, inverse, gain_row):
    scaled = incoming * gain_row
    first_mean = jnp.mean(scaled, axis=-1, keepdims=True)
    second_mean = jnp.mean(scaled * unit_rows, axis=-1, keepdims=True)
    result = inverse * (scaled - first_mean - unit_rows * second_mean)
    return (result, jnp.sum(incoming * unit_rows, axis=0), jnp.sum(incoming, axis=0))


class Place:
    def __init__(self):
        self.z = lax.axis_index("z")
        self.y = lax.axis_index("y")
        self.x = lax.axis_index("x")
        self.c = lax.axis_index("c")

    def to(self, which):
        if which == "x":
            return {"x": 1 - self.x}
        if which == "y":
            return {"y": 1 - self.y}
        if which == "c":
            return {"c": 1 - self.c}
        if which == "z1":
            return {"z": self.z + 1 - 2 * lax.rem(self.z, 2)}
        if which == "z2":
            return {"z": lax.rem(self.z + 2, RING)}
        if which == "down":
            return {"z": lax.rem(self.z + RING - 1, RING)}
        return {"z": lax.rem(self.z + 1, RING)}

    def ring(self, step):
        return lax.rem(self.z + step, RING)


def greet(place, names):
    barrier = pltpu.get_barrier_semaphore()
    for name in names:
        pl.semaphore_signal(barrier, inc=1, device_id=place.to(name), device_id_type=MESH)
    pl.semaphore_wait(barrier, len(names))


class Copies:
    def __init__(self, send_sems, recv_sems):
        self.send_sems, self.recv_sems = send_sems, recv_sems
        self.made = []

    def start(self, place, src, dst, which):
        at = len(self.made)
        copy = pltpu.make_async_remote_copy(
            src_ref=src,
            dst_ref=dst,
            send_sem=self.send_sems.at[at],
            recv_sem=self.recv_sems.at[at],
            device_id=place.to(which),
            device_id_type=MESH,
        )
        copy.start()
        self.made.append(copy)
        return copy

    def finish(self):
        for copy in self.made:
            copy.wait_send()


GATHER_ORDERS = ("xzy", "yzx", "zyx", "zxy")


def gather_unit(order, place, own, whole, base, rows, cols, copies):
    x, y = place.x, place.y

    def at(step, both_y, both_x):
        first = place.ring(step) * 2
        row = first * rows if both_y else (first + y) * rows
        col = base if both_x else base + x * cols
        return whole.at[
            pl.ds(pl.multiple_of(row, rows), rows * (2 if both_y else 1)),
            pl.ds(pl.multiple_of(col, LANES), cols * (2 if both_x else 1)),
        ]

    def send(where, which):
        return copies.start(place, where, where, which)

    arrived = {}
    mine = at(0, False, False)
    if order in ("xzy", "yzx"):
        axis, last = order[0], order[2]
        wide = dict(both_y=axis == "y", both_x=axis == "x")
        first = copies.start(place, own, mine, axis)
        yield
        first.wait_recv()
        hop = send(at(0, **wide), "down")
        ends = [send(at(0, **wide), last)]
        yield
        for step in range(1, RING):
            hop.wait_recv()
            if step < RING - 1:
                hop = send(at(step, **wide), "down")
            ends.append(send(at(step, **wide), last))
            yield
        for copy in ends:
            copy.wait_recv()
    else:
        mid, last = order[1], order[2]
        wide = dict(both_y=mid == "y", both_x=mid == "x")
        hop = copies.start(place, own, mine, "down")
        mids = [copies.start(place, own, mine, mid)]
        ends = []
        yield
        for step in range(1, RING + 1):
            if step < RING:
                hop.wait_recv()
                if step < RING - 1:
                    hop = send(at(step, False, False), "down")
                mids.append(send(at(step, False, False), mid))
            mids[step - 1].wait_recv()
            ends.append(send(at(step - 1, **wide), last))
            yield
        for copy in ends:
            copy.wait_recv()
    del arrived


def run_staggered(makers, spacing):
    waiting = list(makers)
    running = []
    level = 0
    while waiting or running:
        if waiting and level % spacing == 0:
            running.extend(waiting.pop(0))
        still = []
        for unit in running:
            try:
                next(unit)
                still.append(unit)
            except StopIteration:
                pass
        running = still
        level += 1


N_ROWS_COPIES = 8


def gather_kernel(sizes, *refs):
    rows, cols, units_of = sizes
    n_weights = len(units_of)
    h_own, g_own, enc_own = refs[:3]
    own = refs[3 : 3 + n_weights]
    outs = refs[3 + n_weights :]
    h_all, g_all, enc_all = outs[:3]
    whole = outs[3 : 3 + n_weights]
    send_sems, recv_sems, local_sems = outs[3 + n_weights :]
    place = Place()
    greet(place, ("x", "y", "c", "down", "up"))
    copies = Copies(send_sems, recv_sems)
    x, c = place.x, place.c
    n = h_own.shape[0]
    e = enc_own.shape[0]

    def h_at(xx, cc):
        return h_all.at[pl.ds(pl.multiple_of((xx * 2 + cc) * n, 16), n)]

    def e_at(xx, cc):
        return enc_all.at[pl.ds(pl.multiple_of((xx * 2 + cc) * e, 16), e)]

    g_at = g_all.at[pl.ds(pl.multiple_of(c * n, 16), n)]
    hx = copies.start(place, h_own, h_at(x, c), "x")
    hc = copies.start(place, h_own, h_at(x, c), "c")
    local = []

    def keep(src, dst):
        copy = pltpu.make_async_copy(src, dst, local_sems.at[len(local)])
        copy.start()
        local.append(copy)

    keep(h_own, h_at(x, c))
    keep(g_own, g_at)
    keep(enc_own, e_at(x, c))
    groups, group = [], []
    mine = []
    for which, count in enumerate(units_of):
        for unit in range(count):
            base = unit * 2 * cols
            src = own[which].at[unit]
            dst = whole[which].at[
                pl.ds(pl.multiple_of((place.z * 2 + place.y) * rows, rows), rows),
                pl.ds(pl.multiple_of(base + x * cols, LANES), cols),
            ]
            mine.append((src, dst))
            order = GATHER_ORDERS[len(group)]
            group.append(gather_unit(order, place, src, whole[which], base, rows, cols, copies))
            if len(group) == len(GATHER_ORDERS):
                groups.append(group)
                group = []
    for src, dst in mine:
        keep(src, dst)
    for copy in local:
        copy.wait()
    gc = copies.start(place, g_own, g_at, "c")
    ex = copies.start(place, enc_own, e_at(x, c), "x")
    ec = copies.start(place, enc_own, e_at(x, c), "c")

    def rows_unit():
        yield
        yield
        hx.wait_recv()
        hxc = copies.start(place, h_at(1 - x, c), h_at(1 - x, c), "c")
        ex.wait_recv()
        exc = copies.start(place, e_at(1 - x, c), e_at(1 - x, c), "c")
        yield
        for copy in (hc, gc, ec, hxc, exc):
            copy.wait_recv()

    groups[0].append(rows_unit())
    run_staggered(groups, 3)
    copies.finish()


def gather_weights(h_own, g_own, enc_own, shards):
    units_of = tuple(s.shape[0] for s in shards)
    rows, cols = shards[0].shape[1:]
    depth = rows * RING * 2
    n, e, width = h_own.shape[0], enc_own.shape[0], h_own.shape[1]
    n_units = sum(units_of)
    n_copies = N_ROWS_COPIES + n_units * 11
    any_spec = pl.BlockSpec(memory_space=pl.ANY)
    out_shape = [
        jax.ShapeDtypeStruct((4 * n, width), low_type),
        jax.ShapeDtypeStruct((2 * n, width), low_type),
        jax.ShapeDtypeStruct((4 * e, width), low_type),
    ] + [jax.ShapeDtypeStruct((depth, 2 * cols * k), low_type) for k in units_of]
    return pl.pallas_call(
        functools.partial(gather_kernel, (rows, cols, units_of)),
        out_shape=out_shape,
        in_specs=[any_spec] * (3 + len(shards)),
        out_specs=[any_spec] * len(out_shape),
        scratch_shapes=[
            pltpu.SemaphoreType.DMA((n_copies,)),
            pltpu.SemaphoreType.DMA((n_copies,)),
            pltpu.SemaphoreType.DMA((3 + n_units,)),
        ],
        compiler_params=pltpu.CompilerParams(collective_id=0, has_side_effects=True),
        name="gather_weights",
    )(h_own, g_own, enc_own, *shards)


REDUCE_ORDERS = ("xyz", "xzy", "yxz", "yzx")
CHUNK_ORDER = tuple(range(1, RING)) + (0,)


def reduce_unit(order, place, part, base, rows, cols, recv, out, copies):
    x, y = place.x, place.y

    def at(step, row_of, col_of):
        first = place.ring(step) * 2
        row = first * rows if row_of is None else (first + row_of) * rows
        col = base if col_of is None else base + col_of * cols
        return part.at[
            pl.ds(pl.multiple_of(row, rows), rows * (2 if row_of is None else 1)),
            pl.ds(pl.multiple_of(col, LANES), cols * (2 if col_of is None else 1)),
        ]

    used = [0]

    def landing(shape):
        height = shape[0] * (shape[1] // cols)
        where = [
            recv.at[pl.ds(used[0] + k * shape[0], shape[0])] for k in range(shape[1] // cols)
        ]
        used[0] += height
        return where

    def pieces(where, shape):
        return where

    def add(target, source):
        target[...] = (target[...].astype(f32) + source[...].astype(f32)).astype(low_type)

    def exchange(step, which, mid):
        sent = []
        if which == "x":
            if mid:
                spots = [(at(step, y, 1 - x), at(step, y, x))]
            else:
                spots = [(at(step, None, 1 - x), at(step, None, x))]
        else:
            if mid:
                spots = [(at(step, 1 - y, x), at(step, y, x))]
            else:
                spots = [(at(step, 1 - y, k), at(step, y, k)) for k in range(2)]
        for src, keep_at in spots:
            (land,) = landing((src.shape[0], cols))
            sent.append((copies.start(place, src, land, which), keep_at, land))
        return sent

    def take(sent):
        for copy, keep_at, land in sent:
            copy.wait_recv()
            add(keep_at, land)

    first, middle, last = order
    outer = {s: exchange(s, first, False) for s in CHUNK_ORDER}
    yield
    if last == "z":
        inner = {}
        hop = None
        for k, step in enumerate(CHUNK_ORDER):
            take(outer[step])
            inner[step] = exchange(step, middle, True)
            yield
        for step in CHUNK_ORDER:
            take(inner[step])
            if hop is not None:
                copy, land = hop
                copy.wait_recv()
                if step == 0:
                    total = at(0, y, x)[...].astype(f32) + land[...].astype(f32)
                    out[...] = total
                else:
                    add(at(step, y, x), land)
            if step != 0:
                (land,) = landing((rows, cols))
                hop = (copies.start(place, at(step, y, x), land, "down"), land)
                yield
    else:
        hop = None
        for step in CHUNK_ORDER:
            take(outer[step])
            if first == "x":
                spots = [at(step, None, x)]
            else:
                spots = [at(step, y, k) for k in range(2)]
            if hop is not None:
                for (copy, land), spot in zip(hop, spots):
                    copy.wait_recv()
                    add(spot, land)
            if step != 0:
                hop = []
                for spot in spots:
                    (land,) = landing((spot.shape[0], cols))
                    hop.append((copies.start(place, spot, land, "down"), land))
                yield
        src = at(0, 1 - y, x) if last == "y" else at(0, y, 1 - x)
        (land,) = landing((rows, cols))
        copy = copies.start(place, src, land, last)
        yield
        copy.wait_recv()
        out[...] = at(0, y, x)[...].astype(f32) + land[...].astype(f32)


def reduce_kernel(sizes, *refs):
    rows, cols, units_of = sizes
    n_weights = len(units_of)
    small = refs[0]
    parts = refs[1 : 1 + n_weights]
    outs = refs[1 + n_weights :]
    small_out = outs[0]
    sums = outs[1 : 1 + n_weights]
    recv, small_recv, send_sems, recv_sems = outs[1 + n_weights :]
    place = Place()
    greet(place, ("x", "y", "c", "down", "up", "z2"))
    copies = Copies(send_sems, recv_sems)
    groups, group = [], []
    index = 0
    for which, count in enumerate(units_of):
        for unit in range(count):
            order = REDUCE_ORDERS[len(group)]
            group.append(
                reduce_unit(
                    order,
                    place,
                    parts[which],
                    unit * 2 * cols,
                    rows,
                    cols,
                    recv.at[index],
                    sums[which].at[unit],
                    copies,
                )
            )
            index += 1
            if len(group) == len(REDUCE_ORDERS):
                groups.append(group)
                group = []

    def small_unit():
        small_out[0] = small[...]
        for at, which in enumerate(("c", "x", "y", "z1", "z2")):
            copy = copies.start(place, small_out.at[at], small_recv.at[at], which)
            yield
            copy.wait_recv()
            small_out[at + 1] = small_out[at] + small_recv[at]

    groups[0].append(small_unit())
    run_staggered(groups, 3)
    copies.finish()


def reduce_grads(small, parts, rows, cols):
    units_of = tuple(p.shape[1] // (2 * cols) for p in parts)
    n_units = sum(units_of)
    vmem = pl.BlockSpec(memory_space=pltpu.VMEM)
    out_shape = [jax.ShapeDtypeStruct((6,) + small.shape, f32)] + [
        jax.ShapeDtypeStruct((k, rows, cols), f32) for k in units_of
    ]
    n_copies = 5 + n_units * 15
    return pl.pallas_call(
        functools.partial(reduce_kernel, (rows, cols, units_of)),
        out_shape=out_shape,
        in_specs=[vmem] * (1 + len(parts)),
        out_specs=[vmem] * len(out_shape),
        scratch_shapes=[
            pltpu.VMEM((n_units, rows * 15, cols), low_type),
            pltpu.VMEM((5,) + small.shape, f32),
            pltpu.SemaphoreType.DMA((n_copies,)),
            pltpu.SemaphoreType.DMA((n_copies,)),
        ],
        input_output_aliases={},
        compiler_params=pltpu.CompilerParams(
            collective_id=1, has_side_effects=True, vmem_limit_bytes=52 * MIB
        ),
        name="reduce_grads",
    )(small, *parts)


BLOCK = 256


def split_heads(values_in):
    lane = lax.broadcasted_iota(jnp.int32, values_in.shape, 1)
    zero = jnp.zeros_like(values_in)
    return jnp.concatenate(
        [jnp.where(lane < HD, values_in, zero), jnp.where(lane >= HD, values_in, zero)], axis=0
    )


def window_start(place_ref, window, keys):
    if window == keys:
        return 0
    ends = (place_ref[0] + pl.program_id(1) + 1) * BLOCK
    return pl.multiple_of(jnp.maximum(ends - window, 0), BLOCK)


def key_scores(queries, keys, lows, highs, start):
    scores = outer_cols(keys, queries)
    ids = start + lax.broadcasted_iota(jnp.int32, scores.shape, 0)
    lows = jnp.concatenate([lows, lows], axis=1)
    highs = jnp.concatenate([highs, highs], axis=1)
    return jnp.where((ids >= lows) & (ids <= highs), scores, masked_score)


def attend_kernel(window, place_ref, q_ref, k_ref, v_ref, low_ref, high_ref, o_ref, lse_ref):
    start = window_start(place_ref, window, k_ref.shape[0])
    keys = k_ref[pl.ds(start, window)]
    values = v_ref[pl.ds(start, window)]
    queries = split_heads(q_ref[...] * jnp.asarray(HD**-0.5, low_type))
    scores = key_scores(queries, keys, low_ref[...], high_ref[...], start)
    peak = jnp.max(scores, axis=0, keepdims=True)
    probs = jnp.exp(scores - peak)
    total = jnp.sum(probs, axis=0, keepdims=True)
    lse_ref[0, 0] = peak + jnp.log(total)
    context = inner_rows(values, probs.astype(low_type)) / total
    rows = q_ref.shape[0]
    pair = jnp.concatenate([context[:HD, :rows], context[HD:, rows:]], axis=0)
    o_ref[...] = pair.T.astype(low_type)


def attention_specs(rows, keys):
    def block(i, j, p):
        return (j, i)

    def whole(i, j, p):
        return (0, i)

    def line(i, j, p):
        return (0, j)

    q_spec = pl.BlockSpec((BLOCK, PAIR), block)
    k_spec = pl.BlockSpec((keys, PAIR), whole)
    l_spec = pl.BlockSpec((1, BLOCK), line)
    lse_spec = pl.BlockSpec((1, 1, 1, 2 * BLOCK), lambda i, j, p: (i, j, 0, 0))
    return q_spec, k_spec, l_spec, lse_spec


def attend(place, queries, keys, values, lows, highs, window):
    rows, width = queries.shape
    count = keys.shape[0]
    pairs, blocks = width // PAIR, rows // BLOCK
    q_spec, k_spec, l_spec, lse_spec = attention_specs(rows, count)
    cost = pl.CostEstimate(
        flops=8 * rows * window * width,
        bytes_accessed=2 * width * (2 * rows + 2 * count),
        transcendentals=rows * window * width // HD,
    )
    return pl.pallas_call(
        functools.partial(attend_kernel, window),
        out_shape=[
            jax.ShapeDtypeStruct((rows, width), low_type),
            jax.ShapeDtypeStruct((pairs, blocks, 1, 2 * BLOCK), f32),
        ],
        grid_spec=pltpu.PrefetchScalarGridSpec(
            num_scalar_prefetch=1,
            grid=(pairs, blocks),
            in_specs=[q_spec, k_spec, k_spec, l_spec, l_spec],
            out_specs=[q_spec, lse_spec],
        ),
        compiler_params=pltpu.CompilerParams(vmem_limit_bytes=40 * MIB),
        cost_estimate=cost,
        name="attend",
    )(place, queries, keys, values, lows, highs)


def attend_back_kernel(
    window, place_ref, q_ref, k_ref, v_ref, low_ref, high_ref, o_ref, do_ref, lse_ref,
    dq_ref, dk_ref, dv_ref, dk_sum, dv_sum,
):
    scale = jnp.asarray(HD**-0.5, low_type)
    start = window_start(place_ref, window, k_ref.shape[0])
    here = pl.ds(start, window)
    rows = q_ref.shape[0]

    @pl.when(pl.program_id(1) == 0)
    def _():
        dk_sum[...] = jnp.zeros_like(dk_sum)
        dv_sum[...] = jnp.zeros_like(dv_sum)

    keys, values = k_ref[here], v_ref[here]
    queries = split_heads(q_ref[...] * scale)
    grads = split_heads(do_ref[...])
    scores = key_scores(queries, keys, low_ref[...], high_ref[...], start)
    probs = jnp.exp(scores - lse_ref[0, 0])
    grad_probs = outer_cols(values, grads)
    product = (do_ref[...].astype(f32) * o_ref[...].astype(f32)).T
    inner = jnp.concatenate(
        [
            jnp.sum(product[:HD], axis=0, keepdims=True),
            jnp.sum(product[HD:], axis=0, keepdims=True),
        ],
        axis=1,
    )
    grad_scores = (probs * (grad_probs - inner)).astype(low_type)
    dv_sum[here] += matmul(probs.astype(low_type), grads)
    dk_sum[here] += matmul(grad_scores, queries)
    grad_queries = inner_rows(keys, grad_scores) * HD**-0.5
    pair = jnp.concatenate([grad_queries[:HD, :rows], grad_queries[HD:, rows:]], axis=0)
    dq_ref[...] = pair.T.astype(low_type)

    @pl.when(pl.program_id(1) == pl.num_programs(1) - 1)
    def _():
        dk_ref[...] = dk_sum[...].astype(low_type)
        dv_ref[...] = dv_sum[...].astype(low_type)


def attend_back(place, queries, keys, values, lows, highs, context, grads, lse, window):
    rows, width = queries.shape
    count = keys.shape[0]
    pairs, blocks = width // PAIR, rows // BLOCK
    q_spec, k_spec, l_spec, lse_spec = attention_specs(rows, count)
    cost = pl.CostEstimate(
        flops=20 * rows * window * width,
        bytes_accessed=2 * width * (4 * rows + 4 * count),
        transcendentals=rows * window * width // HD,
    )
    return pl.pallas_call(
        functools.partial(attend_back_kernel, window),
        out_shape=[
            jax.ShapeDtypeStruct((rows, width), low_type),
            jax.ShapeDtypeStruct((count, width), low_type),
            jax.ShapeDtypeStruct((count, width), low_type),
        ],
        grid_spec=pltpu.PrefetchScalarGridSpec(
            num_scalar_prefetch=1,
            grid=(pairs, blocks),
            in_specs=[q_spec, k_spec, k_spec, l_spec, l_spec, q_spec, q_spec, lse_spec],
            out_specs=[q_spec, k_spec, k_spec],
            scratch_shapes=[pltpu.VMEM((count, PAIR), f32), pltpu.VMEM((count, PAIR), f32)],
        ),
        compiler_params=pltpu.CompilerParams(vmem_limit_bytes=48 * MIB),
        cost_estimate=cost,
        name="attend_back",
    )(place, queries, keys, values, lows, highs, context, grads, lse)


SWAP = ((0, 1), (1, 0))


def on_device(
    tokens,
    encoder,
    seg_ids,
    enc_lens,
    attn_qkv,
    attn_out,
    cross_q,
    cross_kv,
    cross_out,
    ffn_in,
    ffn_out,
    norm_gains,
    norm_biases,
    out_grad,
):
    outer = lax.axis_size("o")
    core, chip = lax.axis_index("c"), lax.axis_index("x")
    own = tokens.shape[0]
    half = 2 * own
    segment = seg_ids[0]
    seq_len = segment.shape[0]
    cols = cross_q.shape[1]
    width = tokens.shape[1]

    def units(block):
        k = block.shape[-1] // cols
        return block.reshape(block.shape[0], k, cols).transpose(1, 0, 2)

    shards = [
        attn_qkv.astype(low_type),
        attn_out.astype(low_type).T[None],
        cross_q.astype(low_type)[None],
        cross_kv.astype(low_type),
        cross_out.astype(low_type).T[None],
        units(ffn_in.astype(low_type)),
        units(ffn_out.astype(low_type).T),
    ]
    if outer > 1:
        shards = [lax.all_gather(s, "o", axis=1, tiled=True) for s in shards]
    rows = shards[0].shape[1]

    residual = tokens.astype(f32)
    normed, unit_one, inverse_one = norm_forward(residual, norm_gains[0], norm_biases[0])
    rows_one, grads_three, enc_full, *weights = gather_weights(
        normed.astype(low_type), out_grad, encoder[0], shards
    )

    def natural(weight):
        if outer == 1:
            return weight
        parts = weight.reshape(RING, 2, outer, rows // outer, -1)
        return parts.transpose(2, 0, 1, 3, 4).reshape(weight.shape)

    def gathered(weight):
        if outer == 1:
            return weight
        parts = weight.reshape(outer, RING, 2, rows // outer, -1)
        return parts.transpose(1, 2, 0, 3, 4).reshape(weight.shape)

    qkv_w, out_w, query_w, pair_w, back_w, up_w, down_w = map(natural, weights)
    heads_width = 2 * cols

    def half_of(values_in, which):
        return lax.dynamic_slice_in_dim(values_in, which * own, own, 0)

    def core_sum(partial):
        theirs = lax.ppermute(half_of(partial, 1 - core).astype(low_type), "c", SWAP)
        return half_of(partial, core) + theirs.astype(f32)

    def core_rows(mine):
        theirs = lax.ppermute(mine, "c", SWAP)
        return jnp.concatenate(
            [jnp.where(core == 0, mine, theirs), jnp.where(core == 0, theirs, mine)], axis=0
        )

    first = chip * half
    here = lax.dynamic_slice_in_dim(segment, first, half, 0)
    lows = jnp.sum((segment[None, :] < here[:, None]).astype(jnp.int32), axis=1)[None]
    highs = (first + jnp.arange(half, dtype=jnp.int32))[None]
    enc_lows = jnp.zeros_like(highs)
    enc_highs = jnp.broadcast_to(enc_lens[0] - 1, highs.shape)
    place = (chip * (half // BLOCK))[None].astype(jnp.int32)
    window = min(seq_len, seq_len // 2 + BLOCK)

    chip_rows = lax.dynamic_slice_in_dim(rows_one, first, half, 0)
    queries_one = matmul(chip_rows, qkv_w[:, :heads_width]).astype(low_type)
    pair_one = matmul(rows_one, qkv_w[:, heads_width:]).astype(low_type)
    keys_one, values_one = pair_one[:, :heads_width], pair_one[:, heads_width:]
    context_one, lse_one = attend(place, queries_one, keys_one, values_one, lows, highs, window)
    residual_one = residual + core_sum(outer_cols(context_one, out_w))

    normed, unit_two, inverse_two = norm_forward(residual_one, norm_gains[1], norm_biases[1])
    rows_two = core_rows(normed.astype(low_type))
    queries_two = matmul(rows_two, query_w).astype(low_type)
    pair_two = matmul(enc_full, pair_w).astype(low_type)
    keys_two, values_two = pair_two[:, :heads_width], pair_two[:, heads_width:]
    enc_count = enc_full.shape[0]
    context_two, lse_two = attend(
        place, queries_two, keys_two, values_two, enc_lows, enc_highs, enc_count
    )
    residual_two = residual_one + core_sum(outer_cols(context_two, back_w))

    normed, unit_three, inverse_three = norm_forward(residual_two, norm_gains[2], norm_biases[2])
    rows_three = core_rows(normed.astype(low_type))
    inner_pre = matmul(rows_three, up_w)
    sigmoid_pre = jax.nn.sigmoid(inner_pre)
    active = (inner_pre * sigmoid_pre).astype(low_type)
    out_tokens = (residual_two + core_sum(outer_cols(active, down_w))).astype(low_type)

    grad_active = matmul(grads_three, down_w)
    slope = sigmoid_pre * (1.0 + inner_pre * (1.0 - sigmoid_pre))
    grad_inner = (grad_active * slope).astype(low_type)
    down_grad = inner_rows(grads_three, active).astype(low_type)
    up_grad = inner_rows(rows_three, grad_inner).astype(low_type)
    grad_normed = core_sum(outer_cols(grad_inner, up_w))
    grad_residual, gain_three, bias_three = norm_backward(
        grad_normed, unit_three, inverse_three, norm_gains[2]
    )
    grad_total = out_grad.astype(f32) + grad_residual

    grads_two = core_rows(grad_total.astype(low_type))
    grad_context = matmul(grads_two, back_w).astype(low_type)
    back_grad = inner_rows(grads_two, context_two).astype(low_type)
    grad_queries, grad_keys, grad_values = attend_back(
        place, queries_two, keys_two, values_two, enc_lows, enc_highs,
        context_two, grad_context, lse_two, enc_count,
    )
    query_grad = inner_rows(rows_two, grad_queries).astype(low_type)
    grad_pair = jnp.concatenate([grad_keys, grad_values], axis=1)
    pair_grad = inner_rows(enc_full, grad_pair).astype(low_type)
    enc_grad = lax.psum_scatter(
        outer_cols(grad_pair, pair_w).astype(low_type), ("x", "c"), scatter_dimension=0, tiled=True
    ).astype(f32)[None]
    grad_normed = core_sum(outer_cols(grad_queries, query_w))
    grad_residual, gain_two, bias_two = norm_backward(
        grad_normed, unit_two, inverse_two, norm_gains[1]
    )
    grad_total = grad_total + grad_residual

    grads_one = core_rows(grad_total.astype(low_type))
    grad_context = matmul(grads_one, out_w).astype(low_type)
    out_w_grad = inner_rows(grads_one, context_one).astype(low_type)
    grad_queries, grad_keys, grad_values = attend_back(
        place, queries_one, keys_one, values_one, lows, highs,
        context_one, grad_context, lse_one, window,
    )
    grad_pair = jnp.concatenate([grad_keys, grad_values], axis=1)
    qkv_grad = jnp.concatenate(
        [
            inner_rows(chip_rows, grad_queries).astype(low_type),
            inner_rows(rows_one, grad_pair).astype(low_type),
        ],
        axis=1,
    )
    key_term = outer_cols(grad_pair, qkv_w[:, heads_width:])
    query_term = outer_cols(grad_queries, qkv_w[:, :heads_width])
    mine = lax.dynamic_slice_in_dim(key_term, first, half, 0) + query_term
    others = lax.dynamic_slice_in_dim(key_term, (1 - chip) * half, half, 0)
    to_chip = lax.ppermute(core_sum(others).astype(low_type), "x", SWAP)
    grad_normed = core_sum(mine) + to_chip.astype(f32)
    grad_residual, gain_one, bias_one = norm_backward(
        grad_normed, unit_one, inverse_one, norm_gains[0]
    )
    in_grad = grad_total + grad_residual

    small = jnp.stack([gain_one, gain_two, gain_three, bias_one, bias_two, bias_three])
    small = jnp.concatenate([small, jnp.zeros((2, width), f32)], axis=0)
    grads = [up_grad, down_grad, back_grad, query_grad, pair_grad, out_w_grad, qkv_grad]
    small, *sums = reduce_grads(small, [gathered(g) for g in grads], rows, cols)
    small = small[-1]
    if outer > 1:
        small = lax.psum(small, "o")
        sums = [lax.psum_scatter(s, "o", scatter_dimension=1, tiled=True) for s in sums]
    up_sum, down_sum, back_sum, query_sum, pair_sum, out_sum, qkv_sum = sums

    def joined(block):
        return block.transpose(1, 0, 2).reshape(block.shape[1], -1)

    return (
        out_tokens,
        in_grad,
        enc_grad,
        qkv_sum,
        out_sum[0].T,
        query_sum[0],
        pair_sum,
        back_sum[0].T,
        joined(up_sum),
        joined(down_sum).T,
        small[:3],
        small[3:6],
    )


def solution(mesh):
    count, tensor = mesh.devices.shape
    outer = count // (RING * 2)
    fine = Mesh(
        mesh.devices.reshape(outer, RING, 2, tensor // 2, 2), ("o", "z", "y", "x", "c")
    )
    dp, tp = ("o", "z", "y"), ("x", "c")
    in_specs = (
        P(dp + tp, None),
        P(dp, tp, None),
        P(dp, None),
        P(dp),
        P(None, dp, tp),
        P(tp, dp),
        P(dp, tp),
        P(None, dp, tp),
        P(tp, dp),
        P(dp, tp),
        P(tp, dp),
        P(),
        P(),
        P(dp + tp, None),
    )
    out_specs = (
        P(dp + tp, None),
        P(dp + tp, None),
        P(dp, tp, None),
        P(None, dp, tp),
        P(tp, dp),
        P(dp, tp),
        P(None, dp, tp),
        P(tp, dp),
        P(dp, tp),
        P(tp, dp),
        P(),
        P(),
    )
    return jax.shard_map(
        on_device, mesh=fine, in_specs=in_specs, out_specs=out_specs, check_vma=False
    )
```

time: 1470 us -> 658 us (0.45)
  waiting for transfers between devices: 926 us -> 20 us
  Pallas kernels: 0 us -> 475 us
  matrix products: 225 us -> 69.9 us
  blocking collectives: 139 us -> 0 us
  other arithmetic: 84.3 us -> 29.7 us
  loops' own time: 20.1 us -> 0 us
    reduce_scatter x14 -> x1, waiting for transfers between devices: 656 us -> 0.01 us  [on_device(): lax.psum_scatter(outer_cols(grad_pair, pair_w).astype(low_type), ('x', 'c...]
    pallas_call x0 -> x6, Pallas kernels: none -> 475 us  [the longest x1 239 us: gather_weights(): pl.pallas_call(functools.partial(gather_kernel, (rows, cols, units_of)),...]
    all_gather x11 -> x0, waiting for transfers between devices: 268 us -> none  [the longest x3 85.9 us: gather_rows(): return lax.all_gather(values_low, 'tensor', axis=0, tiled=True)]
    dot_general x51 -> x8, matrix products: 168 us -> 23.6 us  [matmul(): return jnp.dot(left, right, preferred_element_type=f32)]
    all_gather x3 -> x0, blocking collectives: 96.2 us -> none  [the longest x1 33.5 us: on_device(): lax.all_gather(attn_out.astype(low_type), 'dp', axis=1, tiled=True)]
    psum x1 -> x0, blocking collectives: 42.7 us -> none  [on_device(): lax.psum((jnp.stack([gain_one, gain_two, gain_three]), jnp.stack([bias_on...]
    convert_element_type x19 -> x8, other arithmetic: 37.6 us -> 8.62 us  [the longest x1 3.38 us: on_device(): grads_two = core_rows(grad_total.astype(low_type))]
    another operation x4 -> x0, loops' own time: 20.1 us -> none  [the longest x2 16 us: attend_back(): lax.scan(one_block, start_totals, indices)]
  transfers between devices with their start and end apart: 25 -> 13, of which waited for: 22 -> 4; matrix products, arithmetic and copies ran while one was open for 13% -> 10% of each run, Pallas kernels for 0% -> 28%
where the time goes in v1:
time: 658 us; the launch traced here: 651 us
  Pallas kernels  475 us (72%)
  matrix products  69.9 us (11%)
  local copies, waits for them, and re-layouts  36.9 us (6%)
  other arithmetic  29.7 us (5%)
  waiting for transfers between devices  20 us (3%)
  between operations  16.2 us (2%)
    pallas_call x1, Pallas kernels, gather_weights(): pl.pallas_call(functools.partial(gather_kernel, (rows, cols, units_of)),...  239 us
    pallas_call x1, Pallas kernels, reduce_grads(): pl.pallas_call(functools.partial(reduce_kernel, (rows, cols, units_of)),...  160 us
    pallas_call x2, Pallas kernels, attend_back(): pl.pallas_call(functools.partial(attend_back_kernel, window), out_shape=[...  45.9 us
    pallas_call x2, Pallas kernels, attend(): pl.pallas_call(functools.partial(attend_kernel, window), out_shape=[jax.S...  31.1 us
    dot_general x8, matrix products, inner_rows(): lax.dot_general(left, right, (((0,), (0,)), ((), ())), preferred_element_...  26.4 us
    unnamed x151, local copies, waits for them, and re-layouts  23.6 us
    dot_general x8, matrix products, matmul(): return jnp.dot(left, right, preferred_element_type=f32)  23.6 us
    dot_general x8, matrix products, outer_cols(): lax.dot_general(left, right, (((1,), (1,)), ((), ())), preferred_element_...  19.8 us
  transfers between devices with their start and end apart: 13, of which 4 were waited for; matrix products, arithmetic and copies ran while one was open for 10% of the time, Pallas kernels for 28%

profile of v1, /device:TPU:0, one launch (start us, length us, event | category | flops | bytes accessed | tf_op | source)
XLA Modules:
  0.0 651.0 jit_solution(17454273067794043186)
XLA Ops:
  18.6 238.5 %gather_weights.1 = (bf16[1536,1024]{1,0:T(8,128)(2,1)}, bf16[768,1024]{1,0:T(8,128)(2,1)}, bf16[1024,1024]{1,0:T(8,128)(2,1)}, bf16[1024,1536]{1,0:T(8,128)(2,1...) custom-call(bf16[384,1024]{1,0:T(8,128)(2,1)} %fusion.10.refs_0_, ...), custom_call_target="tpu_custom_call" | custom-call | tf_op jit(solution)/shard_map/gather_weights/pallas_call | solution.py:275
  257.1 6.1 convolution_convert_fusion.2
  263.3 3.1 convolution_convert_fusion.14.q_ref
  267.6 15.1 %attend.2 = (bf16[768,512]{1,0:T(8,128)(2,1)S(1)}, f32[4,3,1,512]{3,2,1,0:T(1,128)S(1)}) custom-call(s32[1]{0:T(128)} %bitcast.place_ref, bf16[768,512]{1,0:T(8,128)(2,1)S(1)} %copy-done.6, bf16[1536,512]{1,0:T(8,128)(2,1)S(1)} %get-tuple-element.128.k_ref, bf16[1536,512]{1,0:T(8,128)(2,1)S(1)} %get-tuple-element.127.v_ref, ...), custom_call_target="tpu_custom_call" | custom-call | flops 3221225472 | bytes 4718592 | tf_op jit(solution)/shard_map/attend/pallas_call | solution.py:538
  282.8 2.7 fusion.41
  294.4 2.3 convolution_convert_fusion.6
  300.1 16.0 %attend.3 = (bf16[768,512]{1,0:T(8,128)(2,1)S(1)}, f32[4,3,1,512]{3,2,1,0:T(1,128)S(1)}) custom-call(s32[1]{0:T(128)} %bitcast.place_ref, bf16[768,512]{1,0:T(8,128)(2,1)S(1)} %convolution_convert_fusion.13.q_ref, bf16[1024,512]{1,0:T(8,128)(2,1)S(1)} %get-tuple-element.130.k_ref, bf16[1024,512]{1,0:T(8,128)(2,1)S(1)} %get-tuple-element.129.v_ref, ...), custom_call_target="tpu_custom_call" | custom-call | flops 3221225472 | bytes 3670016 | tf_op jit(solution)/shard_map/attend/pallas_call | solution.py:538
  317.4 2.2 collective-permute-done.2
  320.8 2.1 collective-permute-done.3
  323.5 4.0 multiply_convert_fusion.1
  327.6 5.1 multiply_convert_fusion
  332.7 3.4 fusion.44
  338.2 3.4 fusion.43
  344.4 2.6 multiply_reduce_fusion
  347.3 3.4 fusion.34
  351.1 5.1 convolution_convert_fusion.1.refs_1_
  356.2 5.1 convolution_convert_fusion.refs_2_
  364.1 22.2 %attend_back.2 = (bf16[768,512]{1,0:T(8,128)(2,1)S(1)}, bf16[1024,512]{1,0:T(8,128)(2,1)S(1)}, bf16[1024,512]{1,0:T(8,128)(2,1)S(1)}) custom-call(s32[1]{0:T(128)} %bitcast.place_ref, bf16[768,512]{1,0:T(8,128)(2,1)S(1)} %copy-done.9, bf16[1024,512]{1,0:T(8,128)(2,1)} %copy-done.3, bf16[1024,512]{1,0:T(8,128)(2,1)} %copy-done.2, ...), custom_call_target="tpu_custom_call" | custom-call | flops 8053063680 | bytes 7340032 | tf_op jit(solution)/shard_map/attend_back/pallas_call | solution.py:607
  391.6 3.7 convolution_convert_fusion.5
  395.3 3.5 convolution_convert_fusion.10.refs_3_
  405.0 3.7 convolution_convert_fusion.4.refs_5_
  410.2 23.7 %attend_back.3 = (bf16[768,512]{1,0:T(8,128)(2,1)S(1)}, bf16[1536,512]{1,0:T(8,128)(2,1)S(1)}, bf16[1536,512]{1,0:T(8,128)(2,1)}) custom-call(s32[1]{0:T(128)} %bitcast.place_ref, bf16[768,512]{1,0:T(8,128)(2,1)S(1)} %copy-done.7, bf16[1536,512]{1,0:T(8,128)(2,1)} %copy-done.1, bf16[1536,512]{1,0:T(8,128)(2,1)} %copy-done, ...), custom_call_target="tpu_custom_call" | custom-call | flops 8053063680 | bytes 9437184 | tf_op jit(solution)/shard_map/attend_back/pallas_call | solution.py:607
  437.2 3.5 fusion.6
  442.9 4.0 convolution_convert_fusion.3
  449.2 2.0 convolution_convert_fusion.8.refs_6_
  453.1 14.0 %collective-permute-done.11 = bf16[384,1024]{1,0:T(8,128)(2,1)S(1)} collective-permute-done((bf16[384,1024]{1,0:T(8,128)(2,1)S(1)}, bf16[384,1024]{1,0:T(8,128)(2,1)S(1)}, u32[]{:S(2)}, u32[]{:S(2)}) %collective-permute-start.11) | collective-permute-done | bytes 786464 | tf_op jit(solution)/shard_map/ppermute | solution.py:789
  467.2 2.1 fusion.15
  469.4 159.7 %reduce_grads.1 = (f32[6,8,1024]{2,1,0:T(8,128)S(1)}, f32[4,128,256]{2,1,0:T(8,128)S(1)}, f32[4,128,256]{2,1,0:T(8,128)}, f32[1,128,256]{2,1,0:T(8,128)S(1)}, f3...) custom-call(f32[8,1024]{1,0:T(8,128)S(1)} %concatenate.30.refs_0_, ...), custom_call_target="tpu_custom_call" | custom-call | tf_op jit(solution)/shard_map/reduce_grads/pallas_call | solution.py:450
  631.6 2.2 copy.55
  633.7 2.0 copy.52
  636.4 3.1 fusion.14
  639.5 2.1 bitcast_convert_fusion
  (240 shorter events, 62.9 us)
Async XLA Ops:
  7.2 6.1 copy-start.47
  7.2 6.8 %copy-start.45 = (f32[2,128,256]{2,1,0:T(8,128)S(1)}, f32[2,128,256]{2,1,0:T(8,128)}, u32[]{:S(2)}) copy-start(f32[2,128,256]{2,1,0:T(8,128)} %param.21) | copy-start | bytes 786436
  7.2 7.4 %copy-start.48 = (f32[256,128]{1,0:T(8,128)S(1)}, f32[256,128]{1,0:T(8,128)}, u32[]{:S(2)}) copy-start(f32[256,128]{1,0:T(8,128)} %param.22) | copy-start | bytes 393220
  7.2 632.3 %reduce-scatter.2.cloned.1.call-start = ((), (), s32[]{:S(2)}) async-start(), calls=%async_computation.1 | async-start | bytes 2621440 | tf_op jit(solution)/shard_map/reduce_scatter | solution.py:761
  9.0 8.3 %copy-start.49 = (f32[1,1024]{1,0:T(1,128)}, f32[1,1024]{1,0:T(1,128)S(1)}, u32[]{:S(2)}) copy-start(f32[1,1024]{1,0:T(1,128)S(1)} %get-tuple-element.143) | copy-start | bytes 12292
  9.0 6.4 copy-start.39
  10.4 6.9 %copy-start.51 = (f32[384]{0:T(512)}, f32[384]{0:T(512)S(1)}, u32[]{:S(2)}) copy-start(f32[384]{0:T(512)S(1)} %broadcast_multiply_fusion.8) | copy-start | bytes 4612
  257.1 6.1 copy-start.58
  266.7 16.0 %copy-start = (bf16[1536,512]{1,0:T(8,128)(2,1)}, bf16[1536,512]{1,0:T(8,128)(2,1)S(1)}, u32[]{:S(2)}) copy-start(bf16[1536,512]{1,0:T(8,128)(2,1)S(1)} %get-tuple-element.127.v_ref) | copy-start | bytes 4718596
  266.7 16.0 %copy-start.1 = (bf16[1536,512]{1,0:T(8,128)(2,1)}, bf16[1536,512]{1,0:T(8,128)(2,1)S(1)}, u32[]{:S(2)}) copy-start(bf16[1536,512]{1,0:T(8,128)(2,1)S(1)} %get-tuple-element.128.k_ref) | copy-start | bytes 4718596
  267.6 15.2 %copy-start.24 = (bf16[1024,512]{1,0:T(8,128)(2,1)S(1)}, bf16[1024,512]{1,0:T(8,128)(2,1)}, u32[]{:S(2)}) copy-start(bf16[1024,512]{1,0:T(8,128)(2,1)} %get-tuple-element.43) | copy-start | bytes 3145732
  288.0 2.4 collective-permute-start
  292.3 27.3 %copy-start.10 = (f32[384,1024]{1,0:T(8,128)}, f32[384,1024]{1,0:T(8,128)S(1)}, u32[]{:S(2)}) copy-start(f32[384,1024]{1,0:T(8,128)S(1)} %get-tuple-element.126) | copy-start | bytes 4718596
  292.9 4.0 collective-permute-start.1
  300.0 16.1 %copy-start.8 = (bf16[768,512]{1,0:T(8,128)(2,1)}, bf16[768,512]{1,0:T(8,128)(2,1)S(1)}, u32[]{:S(2)}) copy-start(bf16[768,512]{1,0:T(8,128)(2,1)S(1)} %convolution_convert_fusion.13.q_ref) | copy-start | bytes 2359300
  300.1 16.0 %copy-start.27 = (bf16[1024,512]{1,0:T(8,128)(2,1)S(1)}, bf16[1024,512]{1,0:T(8,128)(2,1)}, u32[]{:S(2)}) copy-start(bf16[1024,512]{1,0:T(8,128)(2,1)} %get-tuple-element.48) | copy-start | bytes 3145732
  317.2 2.4 collective-permute-start.2
  320.6 2.4 collective-permute-start.3
  327.6 10.6 %copy-start.66 = (bf16[768,2048]{1,0:T(8,128)(2,1)}, bf16[768,2048]{1,0:T(8,128)(2,1)S(1)}, u32[]{:S(2)}) copy-start(bf16[768,2048]{1,0:T(8,128)(2,1)S(1)} %get-tuple-element.148) | copy-start | bytes 9437188
  337.3 7.1 %collective-permute-start.5 = (bf16[384,1024]{1,0:T(8,128)(2,1)}, bf16[384,1024]{1,0:T(8,128)(2,1)}, u32[]{:S(2)}, u32[]{:S(2)}) collective-permute-start(bf16[384,1024]{1,0:T(8,128)(2,1)} %dynamic-slice_convert_fusion.3), channel_id=1, source_target_pairs={{0,1},{1,0},{2,3},{3,2},{4,5},{5,4},{6,7},{7,6},{8,9},{9,8},{10,11... | collective-permute-start | bytes 2359304 | tf_op jit(solution)/shard_map/ppermute | solution.py:697
  344.3 2.8 collective-permute-start.4
  350.7 10.6 %collective-permute-start.6 = (bf16[384,1024]{1,0:T(8,128)(2,1)S(1)}, bf16[384,1024]{1,0:T(8,128)(2,1)S(1)}, u32[]{:S(2)}, u32[]{:S(2)}) collective-permute-start(bf16[384,1024]{1,0:T(8,128)(2,1)S(1)} %get-tuple-element.120), channel_id=1, source_target_pairs={{0,1},{1,0},{2,3},{3,2},{4,5},{5,4},{6,7},{7,6},{8,9},{9,8},{10,11... | collective-permute-start | bytes 2359304 | tf_op jit(solution)/shard_map/ppermute | solution.py:701
  364.1 22.2 %copy-start.26 = (bf16[1024,512]{1,0:T(8,128)(2,1)S(1)}, bf16[1024,512]{1,0:T(8,128)(2,1)}, u32[]{:S(2)}) copy-start(bf16[1024,512]{1,0:T(8,128)(2,1)} %get-tuple-element.44) | copy-start | bytes 3145732
  388.6 10.3 %collective-permute-start.7 = (bf16[384,1024]{1,0:T(8,128)(2,1)}, bf16[384,1024]{1,0:T(8,128)(2,1)S(1)}, u32[]{:S(2)}, u32[]{:S(2)}) collective-permute-start(bf16[384,1024]{1,0:T(8,128)(2,1)} %dynamic-slice_convert_fusion.2), channel_id=1, source_target_pairs={{0,1},{1,0},{2,3},{3,2},{4,5},{5,4},{6,7},{7,6},{8,9},{9,8},{10,11... | collective-permute-start | bytes 2359304 | tf_op jit(solution)/shard_map/ppermute | solution.py:697
  402.1 6.6 %collective-permute-start.8 = (bf16[384,1024]{1,0:T(8,128)(2,1)S(1)}, bf16[384,1024]{1,0:T(8,128)(2,1)S(1)}, u32[]{:S(2)}, u32[]{:S(2)}) collective-permute-start(bf16[384,1024]{1,0:T(8,128)(2,1)S(1)} %get-tuple-element.117), channel_id=1, source_target_pairs={{0,1},{1,0},{2,3},{3,2},{4,5},{5,4},{6,7},{7,6},{8,9},{9,8},{10,11... | collective-permute-start | bytes 2359304 | tf_op jit(solution)/shard_map/ppermute | solution.py:701
  440.9 6.0 collective-permute-start.10
  442.1 11.0 %collective-permute-start.9 = (bf16[384,1024]{1,0:T(8,128)(2,1)S(1)}, bf16[384,1024]{1,0:T(8,128)(2,1)S(1)}, u32[]{:S(2)}, u32[]{:S(2)}) collective-permute-start(bf16[384,1024]{1,0:T(8,128)(2,1)S(1)} %dynamic-slice_convert_fusion.1), channel_id=1, source_target_pairs={{0,1},{1,0},{2,3},{3,2},{4,5},{5,4},{6,7},{7,6},{8,9},{9,8},{10,11... | collective-permute-start | bytes 2359304 | tf_op jit(solution)/shard_map/ppermute | solution.py:697
  447.2 20.0 %collective-permute-start.11 = (bf16[384,1024]{1,0:T(8,128)(2,1)S(1)}, bf16[384,1024]{1,0:T(8,128)(2,1)S(1)}, u32[]{:S(2)}, u32[]{:S(2)}) collective-permute-start(bf16[384,1024]{1,0:T(8,128)(2,1)S(1)} %add_convert_fusion), channel_id=1, source_target_pairs={{0,2},{2,0},{1,3},{3,1},{4,6},{6,4},{5,7},{7,5},{8,10},{10,8},{9,1... | collective-permute-start | bytes 2359304 | tf_op jit(solution)/shard_map/ppermute | solution.py:789
  451.2 15.9 %copy-start.14 = (bf16[384,1024]{1,0:T(8,128)(2,1)S(1)}, bf16[384,1024]{1,0:T(8,128)(2,1)}, u32[]{:S(2)}) copy-start(bf16[384,1024]{1,0:T(8,128)(2,1)} %param.14) | copy-start | bytes 2359300
  451.2 15.9 %copy-start.50 = (f32[1,1024]{1,0:T(1,128)S(1)}, f32[1,1024]{1,0:T(1,128)}, u32[]{:S(2)}) copy-start(f32[1,1024]{1,0:T(1,128)} %copy-done.49) | copy-start | bytes 12292
  451.2 15.9 %copy-start.52 = (f32[384]{0:T(512)S(1)}, f32[384]{0:T(512)}, u32[]{:S(2)}) copy-start(f32[384]{0:T(512)} %copy-done.51) | copy-start | bytes 4612
  451.2 15.9 %copy-start.54 = (f32[384]{0:T(512)S(1)}, f32[384]{0:T(512)}, u32[]{:S(2)}) copy-start(f32[384]{0:T(512)} %copy-done.53) | copy-start | bytes 4612
  (51 other events, 147.8 us)
Sparse Core Ops, SparseCore 0:
  395.4 30.8 reduce-scatter.1

commit v2 on v1

--- a/solution.py
+++ b/solution.py
@@ -163,128 +163,322 @@
     del arrived
 
 
-def run_staggered(makers, spacing):
-    waiting = list(makers)
-    running = []
-    level = 0
-    while waiting or running:
-        if waiting and level % spacing == 0:
-            running.extend(waiting.pop(0))
-        still = []
-        for unit in running:
-            try:
-                next(unit)
-                still.append(unit)
-            except StopIteration:
-                pass
-        running = still
-        level += 1
-
-
-N_ROWS_COPIES = 8
-
-
-def gather_kernel(sizes, *refs):
+class Levels:
+    def __init__(self, groups, spacing=3):
+        self.groups = [list(g) for g in groups]
+        self.live = [list(g) for g in groups]
+        self.spacing = spacing
+        self.level = 0
+        self.started = 0
+
+    def step(self):
+        if self.started < len(self.groups) and self.level % self.spacing == 0:
+            self.started += 1
+        for group in self.live[: self.started]:
+            for unit in list(group):
+                try:
+                    next(unit)
+                except StopIteration:
+                    group.remove(unit)
+        self.level += 1
+
+    def until(self, group):
+        while self.live[group]:
+            self.step()
+
+    def drain(self):
+        for group in range(len(self.groups)):
+            self.until(group)
+
+
+class Locals:
+    def __init__(self, sems):
+        self.sems, self.made = sems, []
+
+    def start(self, src, dst):
+        copy = pltpu.make_async_copy(src, dst, self.sems.at[len(self.made)])
+        copy.start()
+        self.made.append(copy)
+        return copy
+
+    def finish(self):
+        for copy in self.made:
+            copy.wait()
+
+
+def gather_groups(place, sizes, own, whole, copies, local, orders):
     rows, cols, units_of = sizes
-    n_weights = len(units_of)
-    h_own, g_own, enc_own = refs[:3]
-    own = refs[3 : 3 + n_weights]
-    outs = refs[3 + n_weights :]
-    h_all, g_all, enc_all = outs[:3]
-    whole = outs[3 : 3 + n_weights]
-    send_sems, recv_sems, local_sems = outs[3 + n_weights :]
-    place = Place()
-    greet(place, ("x", "y", "c", "down", "up"))
-    copies = Copies(send_sems, recv_sems)
-    x, c = place.x, place.c
-    n = h_own.shape[0]
-    e = enc_own.shape[0]
-
-    def h_at(xx, cc):
-        return h_all.at[pl.ds(pl.multiple_of((xx * 2 + cc) * n, 16), n)]
-
-    def e_at(xx, cc):
-        return enc_all.at[pl.ds(pl.multiple_of((xx * 2 + cc) * e, 16), e)]
-
-    g_at = g_all.at[pl.ds(pl.multiple_of(c * n, 16), n)]
-    hx = copies.start(place, h_own, h_at(x, c), "x")
-    hc = copies.start(place, h_own, h_at(x, c), "c")
-    local = []
-
-    def keep(src, dst):
-        copy = pltpu.make_async_copy(src, dst, local_sems.at[len(local)])
-        copy.start()
-        local.append(copy)
-
-    keep(h_own, h_at(x, c))
-    keep(g_own, g_at)
-    keep(enc_own, e_at(x, c))
     groups, group = [], []
-    mine = []
+    index = 0
     for which, count in enumerate(units_of):
         for unit in range(count):
             base = unit * 2 * cols
             src = own[which].at[unit]
-            dst = whole[which].at[
-                pl.ds(pl.multiple_of((place.z * 2 + place.y) * rows, rows), rows),
-                pl.ds(pl.multiple_of(base + x * cols, LANES), cols),
-            ]
-            mine.append((src, dst))
-            order = GATHER_ORDERS[len(group)]
-            group.append(gather_unit(order, place, src, whole[which], base, rows, cols, copies))
-            if len(group) == len(GATHER_ORDERS):
+            local.start(
+                src,
+                whole[which].at[
+                    pl.ds(pl.multiple_of((place.z * 2 + place.y) * rows, rows), rows),
+                    pl.ds(pl.multiple_of(base + place.x * cols, LANES), cols),
+                ],
+            )
+            group.append(
+                gather_unit(
+                    orders[index], place, src, whole[which], base, rows, cols, copies
+                )
+            )
+            index += 1
+            if len(group) == 4:
                 groups.append(group)
                 group = []
-    for src, dst in mine:
-        keep(src, dst)
-    for copy in local:
-        copy.wait()
-    gc = copies.start(place, g_own, g_at, "c")
-    ex = copies.start(place, enc_own, e_at(x, c), "x")
-    ec = copies.start(place, enc_own, e_at(x, c), "c")
+    return groups
+
+
+def first_kernel(sizes, orders, *refs):
+    n_weights = len(sizes[2])
+    h_own, *own = refs[: 1 + n_weights]
+    h_all, *whole = refs[1 + n_weights : 2 + 2 * n_weights]
+    send_sems, recv_sems, local_sems = refs[2 + 2 * n_weights :]
+    place = Place()
+    greet(place, ("x", "y", "c", "down", "up"))
+    copies = Copies(send_sems, recv_sems)
+    local = Locals(local_sems)
+    x, c = place.x, place.c
+    n = h_own.shape[0]
+
+    def h_at(xx, cc):
+        return h_all.at[pl.ds(pl.multiple_of((xx * 2 + cc) * n, 16), n)]
+
+    hx = copies.start(place, h_own, h_at(x, c), "x")
+    hc = copies.start(place, h_own, h_at(x, c), "c")
+    local.start(h_own, h_at(x, c))
+    groups = gather_groups(place, sizes, own, whole, copies, local, orders)
+    local.finish()
 
     def rows_unit():
         yield
         yield
         hx.wait_recv()
         hxc = copies.start(place, h_at(1 - x, c), h_at(1 - x, c), "c")
-        ex.wait_recv()
-        exc = copies.start(place, e_at(1 - x, c), e_at(1 - x, c), "c")
-        yield
-        for copy in (hc, gc, ec, hxc, exc):
-            copy.wait_recv()
+        yield
+        yield
+        hc.wait_recv()
+        hxc.wait_recv()
 
     groups[0].append(rows_unit())
-    run_staggered(groups, 3)
+    Levels(groups).drain()
     copies.finish()
 
 
-def gather_weights(h_own, g_own, enc_own, shards):
+ANY_SPEC = pl.BlockSpec(memory_space=pl.ANY)
+VMEM_SPEC = pl.BlockSpec(memory_space=pltpu.VMEM)
+
+
+def gather_shapes(shards):
     units_of = tuple(s.shape[0] for s in shards)
     rows, cols = shards[0].shape[1:]
     depth = rows * RING * 2
-    n, e, width = h_own.shape[0], enc_own.shape[0], h_own.shape[1]
-    n_units = sum(units_of)
-    n_copies = N_ROWS_COPIES + n_units * 11
-    any_spec = pl.BlockSpec(memory_space=pl.ANY)
-    out_shape = [
-        jax.ShapeDtypeStruct((4 * n, width), low_type),
-        jax.ShapeDtypeStruct((2 * n, width), low_type),
-        jax.ShapeDtypeStruct((4 * e, width), low_type),
-    ] + [jax.ShapeDtypeStruct((depth, 2 * cols * k), low_type) for k in units_of]
+    shapes = [jax.ShapeDtypeStruct((depth, 2 * cols * k), low_type) for k in units_of]
+    return (rows, cols, units_of), shapes
+
+
+def gather_first(h_own, shards):
+    sizes, shapes = gather_shapes(shards)
+    n, width = h_own.shape
+    n_units = sum(sizes[2])
+    n_copies = 3 + n_units * 11
+    out_shape = [jax.ShapeDtypeStruct((4 * n, width), low_type)] + shapes
     return pl.pallas_call(
-        functools.partial(gather_kernel, (rows, cols, units_of)),
+        functools.partial(first_kernel, sizes, ("xzy", "zxy", "yzx", "xzy")),
         out_shape=out_shape,
-        in_specs=[any_spec] * (3 + len(shards)),
-        out_specs=[any_spec] * len(out_shape),
+        in_specs=[ANY_SPEC] * (1 + len(shards)),
+        out_specs=[VMEM_SPEC] * len(out_shape),
         scratch_shapes=[
             pltpu.SemaphoreType.DMA((n_copies,)),
             pltpu.SemaphoreType.DMA((n_copies,)),
-            pltpu.SemaphoreType.DMA((3 + n_units,)),
+            pltpu.SemaphoreType.DMA((1 + n_units,)),
         ],
-        compiler_params=pltpu.CompilerParams(collective_id=0, has_side_effects=True),
-        name="gather_weights",
-    )(h_own, g_own, enc_own, *shards)
+        compiler_params=pltpu.CompilerParams(
+            collective_id=0, has_side_effects=True, vmem_limit_bytes=30 * MIB
+        ),
+        name="gather_first",
+    )(h_own, *shards)
+
+
+def norm_rows(values_in, gain_row, bias_row):
+    return norm_forward(values_in, gain_row, bias_row)[0]
+
+
+def loop_rows(count, tile, body):
+    @pl.loop(0, count // tile)
+    def _(i):
+        body(pl.ds(pl.multiple_of(i * tile, tile), tile))
+
+
+def forward_kernel(sizes, window, *refs):
+    n_weights = len(sizes[2])
+    (
+        q_one, pair_one, out_w, lows, highs, enc_highs, gains, biases, residual, g_own, enc_own,
+        *own,
+    ) = refs[: 11 + n_weights]
+    outs = refs[11 + n_weights : 24 + 2 * n_weights]
+    whole = outs[:n_weights]
+    (
+        g_all, enc_all, context_one, lse_one, residual_one, rows_two, q_two, pair_two, context_two,
+        lse_two, residual_two, rows_three, inner_pre,
+    ) = outs[n_weights:]
+    sent, landed, send_sems, recv_sems, local_sems = refs[24 + 2 * n_weights :]
+    query_w, pair_w, back_w, up_w, _ = whole
+    place = Place()
+    greet(place, ("x", "y", "c", "down", "up"))
+    copies = Copies(send_sems, recv_sems)
+    local = Locals(local_sems)
+    x, c = place.x, place.c
+    n, e = residual.shape[0], enc_own.shape[0]
+    heads_width = q_one.shape[1]
+    mine = pl.ds(pl.multiple_of(c * n, 16), n)
+    others = pl.ds(pl.multiple_of((1 - c) * n, 16), n)
+
+    def e_at(xx, cc):
+        return enc_all.at[pl.ds(pl.multiple_of((xx * 2 + cc) * e, 16), e)]
+
+    ex = copies.start(place, enc_own, e_at(x, c), "x")
+    ec = copies.start(place, enc_own, e_at(x, c), "c")
+    gc = copies.start(place, g_own, g_all.at[mine], "c")
+    local.start(g_own, g_all.at[mine])
+    local.start(enc_own, e_at(x, c))
+    orders = ("xzy", "yzx", "xzy", "zxy") + GATHER_ORDERS * 2
+    groups = gather_groups(place, sizes, own, whole, copies, local, orders)
+    local.finish()
+
+    def enc_unit():
+        yield
+        yield
+        ex.wait_recv()
+        exc = copies.start(place, e_at(1 - x, c), e_at(1 - x, c), "c")
+        yield
+        yield
+        ec.wait_recv()
+        gc.wait_recv()
+        exc.wait_recv()
+
+    groups[0].append(enc_unit())
+    comm = Levels(groups)
+
+    def attention(q_ref, pair_ref, low_of, high_of, o_ref, lse_ref, span):
+        keys_count = pair_ref.shape[0]
+        for pair in range(heads_width // PAIR):
+            comm.step()
+            lanes = pl.ds(pair * PAIR, PAIR)
+            value_lanes = pl.ds(heads_width + pair * PAIR, PAIR)
+
+            @pl.loop(0, q_ref.shape[0] // BLOCK)
+            def _(block):
+                rows = pl.ds(pl.multiple_of(block * BLOCK, BLOCK), BLOCK)
+                if span == keys_count:
+                    start = 0
+                else:
+                    ends = (x * (q_ref.shape[0] // BLOCK) + block + 1) * BLOCK
+                    start = pl.multiple_of(jnp.maximum(ends - span, 0), BLOCK)
+                here = pl.ds(start, span)
+                o_ref[rows, lanes], lse_ref[pair, block] = attend_step(
+                    q_ref[rows, lanes],
+                    pair_ref[here, lanes],
+                    pair_ref[here, value_lanes],
+                    low_of(rows),
+                    high_of(rows),
+                    start,
+                )
+
+    def branch(at, context, weight, before, after, gain_at, rows_ref):
+        @pl.loop(0, n // LANES)
+        def _(i):
+            tile = pl.ds(pl.multiple_of(i * LANES, LANES), LANES)
+            theirs = pl.ds(pl.multiple_of((1 - c) * n + i * LANES, LANES), LANES)
+            sent[at, tile] = outer_cols(context[theirs], weight[...]).astype(low_type)
+
+        over = copies.start(place, sent.at[at], landed.at[at], "c")
+
+        @pl.loop(0, n // LANES)
+        def _(i):
+            tile = pl.ds(pl.multiple_of(i * LANES, LANES), LANES)
+            own_rows = pl.ds(pl.multiple_of(c * n + i * LANES, LANES), LANES)
+            after[tile] = before[tile] + outer_cols(context[own_rows], weight[...])
+
+        over.wait_recv()
+
+        @pl.loop(0, n // LANES)
+        def _(i):
+            tile = pl.ds(pl.multiple_of(i * LANES, LANES), LANES)
+            own_rows = pl.ds(pl.multiple_of(c * n + i * LANES, LANES), LANES)
+            total = after[tile] + landed[at, tile].astype(f32)
+            after[tile] = total
+            rows_ref[own_rows] = norm_rows(
+                total, gains[gain_at : gain_at + 1], biases[gain_at : gain_at + 1]
+            ).astype(low_type)
+
+        return copies.start(place, rows_ref.at[mine], rows_ref.at[mine], "c")
+
+    attention(q_one, pair_one, lambda r: lows[:, r], lambda r: highs[:, r], context_one, lse_one, window)
+    comm.step()
+    over = branch(0, context_one, out_w, residual, residual_one, 1, rows_two)
+    comm.until(0)
+    loop_rows(enc_all.shape[0], BLOCK, lambda r: store(pair_two, r, matmul(enc_all[r], pair_w[...])))
+    over.wait_recv()
+    comm.step()
+    loop_rows(2 * n, BLOCK, lambda r: store(q_two, r, matmul(rows_two[r], query_w[...])))
+    attention(
+        q_two, pair_two, lambda r: jnp.zeros((1, BLOCK), jnp.int32), lambda r: enc_highs[:, r],
+        context_two, lse_two, enc_all.shape[0],
+    )
+    comm.step()
+    over = branch(1, context_two, back_w, residual_one, residual_two, 2, rows_three)
+    comm.until(1)
+    over.wait_recv()
+    loop_rows(2 * n, LANES, lambda r: store(inner_pre, r, matmul(rows_three[r], up_w[...])))
+    comm.drain()
+    copies.finish()
+
+
+def store(ref, rows, values_in):
+    ref[rows] = values_in.astype(ref.dtype)
+
+
+def forward(q_one, pair_one, out_w, lows, highs, enc_highs, gains, biases, residual, g_own, enc_own, shards, window):
+    sizes, shapes = gather_shapes(shards)
+    n, width = residual.shape
+    e = enc_own.shape[0]
+    hidden = shapes[-1].shape[1]
+    heads_width = q_one.shape[1]
+    n_units = sum(sizes[2])
+    n_copies = 8 + n_units * 11
+    lse = jax.ShapeDtypeStruct((heads_width // PAIR, 2 * n // BLOCK, 1, 2 * BLOCK), f32)
+
+    def low(*shape):
+        return jax.ShapeDtypeStruct(shape, low_type)
+
+    keep = jax.ShapeDtypeStruct((n, width), f32)
+    out_shape = shapes + [
+        low(2 * n, width), low(4 * e, width), low(2 * n, heads_width), lse, keep, low(2 * n, width),
+        low(2 * n, heads_width), low(4 * e, 2 * heads_width), low(2 * n, heads_width), lse, keep,
+        low(2 * n, width), jax.ShapeDtypeStruct((2 * n, hidden), f32),
+    ]
+    return pl.pallas_call(
+        functools.partial(forward_kernel, sizes, window),
+        out_shape=out_shape,
+        in_specs=[VMEM_SPEC] * 9 + [ANY_SPEC] * (2 + len(shards)),
+        out_specs=[VMEM_SPEC] * len(out_shape),
+        scratch_shapes=[
+            pltpu.VMEM((2, n, width), low_type),
+            pltpu.VMEM((2, n, width), low_type),
+            pltpu.SemaphoreType.DMA((n_copies,)),
+            pltpu.SemaphoreType.DMA((n_copies,)),
+            pltpu.SemaphoreType.DMA((2 + n_units,)),
+        ],
+        compiler_params=pltpu.CompilerParams(
+            collective_id=2, has_side_effects=True, vmem_limit_bytes=60 * MIB
+        ),
+        name="forward",
+    )(q_one, pair_one, out_w, lows, highs, enc_highs, gains, biases, residual, g_own, enc_own, *shards)
 
 
 REDUCE_ORDERS = ("xyz", "xzy", "yxz", "yzx")
@@ -435,7 +629,7 @@
             small_out[at + 1] = small_out[at] + small_recv[at]
 
     groups[0].append(small_unit())
-    run_staggered(groups, 3)
+    Levels(groups).drain()
     copies.finish()
 
 
@@ -492,20 +686,16 @@
     return jnp.where((ids >= lows) & (ids <= highs), scores, masked_score)
 
 
-def attend_kernel(window, place_ref, q_ref, k_ref, v_ref, low_ref, high_ref, o_ref, lse_ref):
-    start = window_start(place_ref, window, k_ref.shape[0])
-    keys = k_ref[pl.ds(start, window)]
-    values = v_ref[pl.ds(start, window)]
-    queries = split_heads(q_ref[...] * jnp.asarray(HD**-0.5, low_type))
-    scores = key_scores(queries, keys, low_ref[...], high_ref[...], start)
+def attend_step(q_block, keys, values, lows, highs, start):
+    rows = q_block.shape[0]
+    queries = split_heads(q_block * jnp.asarray(HD**-0.5, low_type))
+    scores = key_scores(queries, keys, lows, highs, start)
     peak = jnp.max(scores, axis=0, keepdims=True)
     probs = jnp.exp(scores - peak)
     total = jnp.sum(probs, axis=0, keepdims=True)
-    lse_ref[0, 0] = peak + jnp.log(total)
     context = inner_rows(values, probs.astype(low_type)) / total
-    rows = q_ref.shape[0]
     pair = jnp.concatenate([context[:HD, :rows], context[HD:, rows:]], axis=0)
-    o_ref[...] = pair.T.astype(low_type)
+    return pair.T.astype(low_type), peak + jnp.log(total)
 
 
 def attention_specs(rows, keys):
@@ -523,34 +713,6 @@
     l_spec = pl.BlockSpec((1, BLOCK), line)
     lse_spec = pl.BlockSpec((1, 1, 1, 2 * BLOCK), lambda i, j, p: (i, j, 0, 0))
     return q_spec, k_spec, l_spec, lse_spec
-
-
-def attend(place, queries, keys, values, lows, highs, window):
-    rows, width = queries.shape
-    count = keys.shape[0]
-    pairs, blocks = width // PAIR, rows // BLOCK
-    q_spec, k_spec, l_spec, lse_spec = attention_specs(rows, count)
-    cost = pl.CostEstimate(
-        flops=8 * rows * window * width,
-        bytes_accessed=2 * width * (2 * rows + 2 * count),
-        transcendentals=rows * window * width // HD,
-    )
-    return pl.pallas_call(
-        functools.partial(attend_kernel, window),
-        out_shape=[
-            jax.ShapeDtypeStruct((rows, width), low_type),
-            jax.ShapeDtypeStruct((pairs, blocks, 1, 2 * BLOCK), f32),
-        ],
-        grid_spec=pltpu.PrefetchScalarGridSpec(
-            num_scalar_prefetch=1,
-            grid=(pairs, blocks),
-            in_specs=[q_spec, k_spec, k_spec, l_spec, l_spec],
-            out_specs=[q_spec, lse_spec],
-        ),
-        compiler_params=pltpu.CompilerParams(vmem_limit_bytes=40 * MIB),
-        cost_estimate=cost,
-        name="attend",
-    )(place, queries, keys, values, lows, highs)
 
 
 def attend_back_kernel(
@@ -627,6 +789,22 @@
 SWAP = ((0, 1), (1, 0))
 
 
+def width_orders(outer, width):
+    def spread(values_in):
+        if outer == 1:
+            return values_in
+        parts = values_in.reshape(values_in.shape[:-1] + (outer, RING * 2, -1))
+        return jnp.swapaxes(parts, -3, -2).reshape(values_in.shape)
+
+    def back(values_in):
+        if outer == 1:
+            return values_in
+        parts = values_in.reshape(values_in.shape[:-1] + (RING * 2, outer, -1))
+        return jnp.swapaxes(parts, -3, -2).reshape(values_in.shape)
+
+    return spread, back
+
+
 def on_device(
     tokens,
     encoder,
@@ -644,6 +822,9 @@
     out_grad,
 ):
     outer = lax.axis_size("o")
+    spread, gathered_back = width_orders(outer, tokens.shape[1])
+    tokens, encoder, out_grad = spread(tokens), spread(encoder[0]), spread(out_grad)
+    norm_gains, norm_biases = spread(norm_gains), spread(norm_biases)
     core, chip = lax.axis_index("c"), lax.axis_index("x")
     own = tokens.shape[0]
     half = 2 * own
@@ -671,23 +852,8 @@
 
     residual = tokens.astype(f32)
     normed, unit_one, inverse_one = norm_forward(residual, norm_gains[0], norm_biases[0])
-    rows_one, grads_three, enc_full, *weights = gather_weights(
-        normed.astype(low_type), out_grad, encoder[0], shards
-    )
-
-    def natural(weight):
-        if outer == 1:
-            return weight
-        parts = weight.reshape(RING, 2, outer, rows // outer, -1)
-        return parts.transpose(2, 0, 1, 3, 4).reshape(weight.shape)
-
-    def gathered(weight):
-        if outer == 1:
-            return weight
-        parts = weight.reshape(outer, RING, 2, rows // outer, -1)
-        return parts.transpose(1, 2, 0, 3, 4).reshape(weight.shape)
-
-    qkv_w, out_w, query_w, pair_w, back_w, up_w, down_w = map(natural, weights)
+    rows_one, qkv_w, out_w = gather_first(normed.astype(low_type), shards[:2])
+
     heads_width = 2 * cols
 
     def half_of(values_in, which):
@@ -715,24 +881,19 @@
     chip_rows = lax.dynamic_slice_in_dim(rows_one, first, half, 0)
     queries_one = matmul(chip_rows, qkv_w[:, :heads_width]).astype(low_type)
     pair_one = matmul(rows_one, qkv_w[:, heads_width:]).astype(low_type)
+    (
+        query_w, pair_w, back_w, up_w, down_w, grads_three, enc_full, context_one, lse_one, residual_one,
+        rows_two, queries_two, pair_two, context_two, lse_two, residual_two, rows_three, inner_pre,
+    ) = forward(
+        queries_one, pair_one, out_w, lows, highs, enc_highs, norm_gains, norm_biases, residual,
+        out_grad, encoder, shards[2:], window,
+    )
+    enc_count = enc_full.shape[0]
     keys_one, values_one = pair_one[:, :heads_width], pair_one[:, heads_width:]
-    context_one, lse_one = attend(place, queries_one, keys_one, values_one, lows, highs, window)
-    residual_one = residual + core_sum(outer_cols(context_one, out_w))
-
-    normed, unit_two, inverse_two = norm_forward(residual_one, norm_gains[1], norm_biases[1])
-    rows_two = core_rows(normed.astype(low_type))
-    queries_two = matmul(rows_two, query_w).astype(low_type)
-    pair_two = matmul(enc_full, pair_w).astype(low_type)
     keys_two, values_two = pair_two[:, :heads_width], pair_two[:, heads_width:]
-    enc_count = enc_full.shape[0]
-    context_two, lse_two = attend(
-        place, queries_two, keys_two, values_two, enc_lows, enc_highs, enc_count
-    )
-    residual_two = residual_one + core_sum(outer_cols(context_two, back_w))
-
-    normed, unit_three, inverse_three = norm_forward(residual_two, norm_gains[2], norm_biases[2])
-    rows_three = core_rows(normed.astype(low_type))
-    inner_pre = matmul(rows_three, up_w)
+    unit_two, inverse_two = norm_forward(residual_one, norm_gains[1], norm_biases[1])[1:]
+    unit_three, inverse_three = norm_forward(residual_two, norm_gains[2], norm_biases[2])[1:]
+
     sigmoid_pre = jax.nn.sigmoid(inner_pre)
     active = (inner_pre * sigmoid_pre).astype(low_type)
     out_tokens = (residual_two + core_sum(outer_cols(active, down_w))).astype(low_type)
@@ -796,7 +957,7 @@
     small = jnp.stack([gain_one, gain_two, gain_three, bias_one, bias_two, bias_three])
     small = jnp.concatenate([small, jnp.zeros((2, width), f32)], axis=0)
     grads = [up_grad, down_grad, back_grad, query_grad, pair_grad, out_w_grad, qkv_grad]
-    small, *sums = reduce_grads(small, [gathered(g) for g in grads], rows, cols)
+    small, *sums = reduce_grads(small, grads, rows, cols)
     small = small[-1]
     if outer > 1:
         small = lax.psum(small, "o")
@@ -807,9 +968,9 @@
         return block.transpose(1, 0, 2).reshape(block.shape[1], -1)
 
     return (
-        out_tokens,
-        in_grad,
-        enc_grad,
+        gathered_back(out_tokens),
+        gathered_back(in_grad),
+        gathered_back(enc_grad),
         qkv_sum,
         out_sum[0].T,
         query_sum[0],
@@ -817,8 +978,8 @@
         back_sum[0].T,
         joined(up_sum),
         joined(down_sum).T,
-        small[:3],
-        small[3:6],
+        gathered_back(small[:3]),
+        gathered_back(small[3:6]),
     )
 
 

time: 658 us -> 580 us (0.88)
  Pallas kernels: 475 us -> 403 us
    pallas_call x3 -> x2, Pallas kernels: 270 us -> 196 us  [the longest x1 135 us: forward(): pl.pallas_call(functools.partial(forward_kernel, sizes, window), out_shap...]
    dot_general x8 -> x5, matrix products: 23.6 us -> 17.8 us  [matmul(): return jnp.dot(left, right, preferred_element_type=f32)]
    unnamed x151 -> x111, local copies, waits for them, and re-layouts: 23.6 us -> 18.6 us
    dot_general x8 -> x6, matrix products: 19.8 us -> 17.9 us  [outer_cols(): lax.dot_general(left, right, (((1,), (1,)), ((), ())), preferred_element_...]
  transfers between devices with their start and end apart: 13 -> 9, of which waited for: 4 -> 1; matrix products, arithmetic and copies ran while one was open for 10% -> 13% of each run, Pallas kernels for 28% -> 32%
where the time goes in v2:
time: 580 us; the launch traced here: 570 us
  Pallas kernels  403 us (69%)
  matrix products  64.7 us (11%)
  local copies, waits for them, and re-layouts  36.4 us (6%)
  other arithmetic  33.1 us (6%)
  between operations  15.6 us (3%)
  waiting for transfers between devices  13.7 us (2%)
    pallas_call x1, Pallas kernels, reduce_grads(): pl.pallas_call(functools.partial(reduce_kernel, (rows, cols, units_of)),...  161 us
    pallas_call x1, Pallas kernels, forward(): pl.pallas_call(functools.partial(forward_kernel, sizes, window), out_shap...  135 us
    pallas_call x1, Pallas kernels, gather_first(): pl.pallas_call(functools.partial(first_kernel, sizes, ('xzy', 'zxy', 'yzx...  61.2 us
    pallas_call x2, Pallas kernels, attend_back(): pl.pallas_call(functools.partial(attend_back_kernel, window), out_shape=[...  45.7 us
    dot_general x8, matrix products, inner_rows(): lax.dot_general(left, right, (((0,), (0,)), ((), ())), preferred_element_...  29 us
    unnamed x111, local copies, waits for them, and re-layouts  18.6 us
    dot_general x6, matrix products, outer_cols(): lax.dot_general(left, right, (((1,), (1,)), ((), ())), preferred_element_...  17.9 us
    dot_general x5, matrix products, matmul(): return jnp.dot(left, right, preferred_element_type=f32)  17.8 us
  transfers between devices with their start and end apart: 9, of which 1 were waited for; matrix products, arithmetic and copies ran while one was open for 13% of the time, Pallas kernels for 32%

profile of v2, /device:TPU:0, one launch (start us, length us, event | category | flops | bytes accessed | tf_op | source)
XLA Modules:
  0.0 569.9 jit_solution(2306246975706471856)
XLA Ops:
  12.5 61.2 %gather_first.1 = (bf16[1536,1024]{1,0:T(8,128)(2,1)S(1)}, bf16[1024,1536]{1,0:T(8,128)(2,1)S(1)}, bf16[1024,512]{1,0:T(8,128)(2,1)S(1)}) custom-call(bf16[384,1024]{1,0:T(8,128)(2,1)S(1)} %add_convert_fusion.2.refs_0_, bf16[3,128,256]{2,1,0:T(8,128)(2,1)S(1)} %convert_element_type.126.refs_1_, bf16[1,128,256]{2,1,0:T(8,128)(2,1)S(1)} %bitcast.80), custom_call_target="tpu_custom_call" | custom-call | tf_op jit(solution)/shard_map/gather_first/pallas_call | solution.py:290
  73.7 4.9 convolution_convert_fusion.2.refs_1_
  78.7 1.9 convolution_convert_fusion.12.refs_0_.q_ref
  89.0 134.8 %forward.1 = (bf16[1024,512]{1,0:T(8,128)(2,1)}, bf16[1024,1024]{1,0:T(8,128)(2,1)}, bf16[1024,512]{1,0:T(8,128)(2,1)}, bf16[1024,2048]{1,0:T(8,128)(2,1)}, bf16...) custom-call(bf16[768,512]{1,0:T(8,128)(2,1)} %convolution_convert_fu, ...), custom_call_target="tpu_custom_call" | custom-call | tf_op jit(solution)/shard_map/forward/pallas_call | solution.py:465
  223.7 9.0 %multiply_convert_fusion = bf16[768,2048]{1,0:T(8,128)(2,1)S(1)} fusion(f32[768,2048]{1,0:T(8,128)} %get-tuple-element.51, bf16[768,1024]{1,0:T(8,128)(2,1)} %get-tuple-element.53, bf16[1024,2048]{1,0:T(8,128)(2,1)} %get-tuple-element.52), kind=kOutput, calls=%fused_computation | convolution fusion | flops 3235381248 | bytes 15204352 | tf_op jit(solution)/shard_map/dot_general | solution.py:24
  234.3 5.1 fusion.20
  239.5 2.4 dynamic-slice_convert_fusion.3
  241.9 4.6 multiply_convert_fusion.1
  246.5 3.5 fusion.19
  252.1 1.8 fusion.16
  253.9 5.1 convolution_convert_fusion.refs_2_
  261.1 3.1 fusion.17
  264.6 2.6 multiply_reduce_fusion
  268.1 3.2 fusion.15
  271.4 7.8 %convolution_convert_fusion.1.refs_1_ = bf16[1024,2048]{1,0:T(8,128)(2,1)} fusion(bf16[768,1024]{1,0:T(8,128)(2,1)} %get-tuple-element.71, bf16[768,2048]{1,0:T(8,128)(2,1)} %copy-done.49), kind=kOutput, calls=%fused_computation.5 | convolution fusion | flops 3223322624 | bytes 8912896 | tf_op jit(solution)/shard_map/dot_general | solution.py:28
  282.2 22.4 %attend_back.2 = (bf16[768,512]{1,0:T(8,128)(2,1)S(1)}, bf16[1024,512]{1,0:T(8,128)(2,1)S(1)}, bf16[1024,512]{1,0:T(8,128)(2,1)S(1)}) custom-call(s32[1]{0:T(128)} %bitcast.15.place_ref, bf16[768,512]{1,0:T(8,128)(2,1)S(1)} %copy-done.12, bf16[1024,512]{1,0:T(8,128)(2,1)} %get-tuple-element.140.k_ref, bf16[1024,512]{1,0:T(8,128)(2,1)} %get-tuple-element.139.v_ref, ...), custom_call_target="tpu_custom_call" | custom-call | flops 8053063680 | bytes 7340032 | tf_op jit(solution)/shard_map/attend_back/pallas_call | solution.py:769
  309.5 3.8 convolution_convert_fusion.5
  313.3 3.6 convolution_convert_fusion.8.refs_4_
  320.0 2.0 convolution_convert_fusion.9.refs_3_
  323.0 3.8 convolution_convert_fusion.4.refs_5_
  329.4 23.3 %attend_back.3 = (bf16[768,512]{1,0:T(8,128)(2,1)S(1)}, bf16[1536,512]{1,0:T(8,128)(2,1)S(1)}, bf16[1536,512]{1,0:T(8,128)(2,1)}) custom-call(s32[1]{0:T(128)} %bitcast.15.place_ref, bf16[768,512]{1,0:T(8,128)(2,1)S(1)} %copy-done.2, bf16[1536,512]{1,0:T(8,128)(2,1)} %get-tuple-element.138.k_ref, bf16[1536,512]{1,0:T(8,128)(2,1)} %get-tuple-element.137.v_ref, ...), custom_call_target="tpu_custom_call" | custom-call | flops 8053063680 | bytes 9437184 | tf_op jit(solution)/shard_map/attend_back/pallas_call | solution.py:769
  355.2 3.5 fusion
  360.8 3.7 convolution_convert_fusion.3
  367.3 2.0 convolution_convert_fusion.7.refs_6_
  369.3 1.9 pad_maximum_fusion.refs_7_
  371.2 13.7 %collective-permute-done.7 = bf16[384,1024]{1,0:T(8,128)(2,1)S(1)} collective-permute-done((bf16[384,1024]{1,0:T(8,128)(2,1)S(1)}, bf16[384,1024]{1,0:T(8,128)(2,1)S(1)}, u32[]{:S(2)}, u32[]{:S(2)}) %collective-permute-start.7) | collective-permute-done | bytes 786464 | tf_op jit(solution)/shard_map/ppermute | solution.py:950
  384.9 2.0 multiply_reduce_fusion.2
  386.9 161.3 %reduce_grads.1 = (f32[6,8,1024]{2,1,0:T(8,128)S(1)}, f32[4,128,256]{2,1,0:T(8,128)S(1)}, f32[4,128,256]{2,1,0:T(8,128)}, f32[1,128,256]{2,1,0:T(8,128)S(1)}, f3...) custom-call(f32[8,1024]{1,0:T(8,128)S(1)} %concatenate.22.refs_0_, ...), custom_call_target="tpu_custom_call" | custom-call | tf_op jit(solution)/shard_map/reduce_grads/pallas_call | solution.py:644
  550.7 2.2 copy.55
  552.9 2.0 copy.52
  555.5 3.1 multiply_add_fusion
  558.6 2.1 bitcast_convert_fusion
  (183 shorter events, 47.0 us)
Async XLA Ops:
  7.2 4.9 slice-start
  7.2 4.9 copy-start.15
  7.2 4.7 copy-start.39
  7.2 551.4 %reduce-scatter.2.cloned.1.call-start = ((), (), s32[]{:S(2)}) async-start(), calls=%async_computation.1 | async-start | bytes 2621440 | tf_op jit(solution)/shard_map/reduce_scatter | solution.py:922
  73.7 5.0 copy-start
  73.7 5.0 copy-start.3
  73.7 5.0 copy-start.8
  80.6 3.8 copy-start.40
  80.6 4.5 copy-start.38
  80.6 5.1 copy-start.41
  80.6 5.9 %copy-start.34 = (f32[128,1024]{1,0:T(8,128)S(1)}, f32[128,1024]{1,0:T(8,128)}, u32[]{:S(2)}) copy-start(f32[128,1024]{1,0:T(8,128)} %param.23) | copy-start | bytes 1572868
  81.2 6.2 %copy-start.35 = (f32[1024,128]{1,0:T(8,128)S(1)}, f32[1024,128]{1,0:T(8,128)}, u32[]{:S(2)}) copy-start(f32[1024,128]{1,0:T(8,128)} %param.24) | copy-start | bytes 1572868
  223.7 10.6 %copy-start.44 = (bf16[1024,2048]{1,0:T(8,128)(2,1)S(1)}, bf16[1024,2048]{1,0:T(8,128)(2,1)}, u32[]{:S(2)}) copy-start(bf16[1024,2048]{1,0:T(8,128)(2,1)} %get-tuple-element.54) | copy-start | bytes 12582916
  241.9 4.6 copy-start.43
  241.9 22.7 %collective-permute-start.1 = (bf16[384,1024]{1,0:T(8,128)(2,1)}, bf16[384,1024]{1,0:T(8,128)(2,1)}, u32[]{:S(2)}, u32[]{:S(2)}) collective-permute-start(bf16[384,1024]{1,0:T(8,128)(2,1)} %dynamic-slice_convert_fusion.3), channel_id=1, source_target_pairs={{0,1},{1,0},{2,3},{3,2},{4,5},{5,4},{6,7},{7,6},{8,9},{9,8},{10,11... | collective-permute-start | bytes 2359304 | tf_op jit(solution)/shard_map/ppermute | solution.py:863
  246.5 5.6 copy-start.19
  250.0 4.0 copy-start.25
  251.1 16.1 %collective-permute-start = (bf16[384,1024]{1,0:T(8,128)(2,1)}, bf16[384,1024]{1,0:T(8,128)(2,1)S(1)}, u32[]{:S(2)}, u32[]{:S(2)}) collective-permute-start(bf16[384,1024]{1,0:T(8,128)(2,1)} %dynamic-slice_convert_fusion.4), channel_id=1, source_target_pairs={{0,1},{1,0},{2,3},{3,2},{4,5},{5,4},{6,7},{7,6},{8,9},{9,8},{10,11... | collective-permute-start | bytes 2359304 | tf_op jit(solution)/shard_map/ppermute | solution.py:863
  253.9 5.1 copy-start.16
  261.1 3.1 copy-start.17
  264.5 3.5 copy-start.24
  264.6 3.5 copy-start.26
  271.3 7.9 %collective-permute-start.2 = (bf16[384,1024]{1,0:T(8,128)(2,1)S(1)}, bf16[384,1024]{1,0:T(8,128)(2,1)S(1)}, u32[]{:S(2)}, u32[]{:S(2)}) collective-permute-start(bf16[384,1024]{1,0:T(8,128)(2,1)S(1)} %get-tuple-element.134), channel_id=1, source_target_pairs={{0,1},{1,0},{2,3},{3,2},{4,5},{5,4},{6,7},{7,6},{8,9},{9,8},{10,11... | collective-permute-start | bytes 2359304 | tf_op jit(solution)/shard_map/ppermute | solution.py:867
  282.2 22.4 %copy-start.28 = (bf16[1024,512]{1,0:T(8,128)(2,1)S(1)}, bf16[1024,512]{1,0:T(8,128)(2,1)}, u32[]{:S(2)}) copy-start(bf16[1024,512]{1,0:T(8,128)(2,1)} %get-tuple-element.62) | copy-start | bytes 3145732
  306.8 10.1 %collective-permute-start.3 = (bf16[384,1024]{1,0:T(8,128)(2,1)}, bf16[384,1024]{1,0:T(8,128)(2,1)S(1)}, u32[]{:S(2)}, u32[]{:S(2)}) collective-permute-start(bf16[384,1024]{1,0:T(8,128)(2,1)} %dynamic-slice_convert_fusion.2), channel_id=1, source_target_pairs={{0,1},{1,0},{2,3},{3,2},{4,5},{5,4},{6,7},{7,6},{8,9},{9,8},{10,11... | collective-permute-start | bytes 2359304 | tf_op jit(solution)/shard_map/ppermute | solution.py:863
  313.3 3.6 copy-start.18
  313.3 3.6 copy-start.21
  320.0 6.8 %collective-permute-start.4 = (bf16[384,1024]{1,0:T(8,128)(2,1)S(1)}, bf16[384,1024]{1,0:T(8,128)(2,1)S(1)}, u32[]{:S(2)}, u32[]{:S(2)}) collective-permute-start(bf16[384,1024]{1,0:T(8,128)(2,1)S(1)} %get-tuple-element.131), channel_id=1, source_target_pairs={{0,1},{1,0},{2,3},{3,2},{4,5},{5,4},{6,7},{7,6},{8,9},{9,8},{10,11... | collective-permute-start | bytes 2359304 | tf_op jit(solution)/shard_map/ppermute | solution.py:867
  358.9 5.7 collective-permute-start.6
  360.2 11.0 %collective-permute-start.5 = (bf16[384,1024]{1,0:T(8,128)(2,1)S(1)}, bf16[384,1024]{1,0:T(8,128)(2,1)S(1)}, u32[]{:S(2)}, u32[]{:S(2)}) collective-permute-start(bf16[384,1024]{1,0:T(8,128)(2,1)S(1)} %dynamic-slice_convert_fusion.1), channel_id=1, source_target_pairs={{0,1},{1,0},{2,3},{3,2},{4,5},{5,4},{6,7},{7,6},{8,9},{9,8},{10,11... | collective-permute-start | bytes 2359304 | tf_op jit(solution)/shard_map/ppermute | solution.py:863
  364.8 20.0 %collective-permute-start.7 = (bf16[384,1024]{1,0:T(8,128)(2,1)S(1)}, bf16[384,1024]{1,0:T(8,128)(2,1)S(1)}, u32[]{:S(2)}, u32[]{:S(2)}) collective-permute-start(bf16[384,1024]{1,0:T(8,128)(2,1)S(1)} %add_convert_fusion), channel_id=1, source_target_pairs={{0,2},{2,0},{1,3},{3,1},{4,6},{6,4},{5,7},{7,5},{8,10},{10,8},{9,1... | collective-permute-start | bytes 2359304 | tf_op jit(solution)/shard_map/ppermute | solution.py:950
  550.7 4.8 copy-start.23
  (28 other events, 47.4 us)
Sparse Core Ops, SparseCore 0:
  313.4 31.1 reduce-scatter.1

commit v3 on v2

--- a/solution.py
+++ b/solution.py
@@ -164,15 +164,18 @@
 
 
 class Levels:
-    def __init__(self, groups, spacing=3):
-        self.groups = [list(g) for g in groups]
+    def __init__(self, groups, spacing=None):
         self.live = [list(g) for g in groups]
         self.spacing = spacing
         self.level = 0
         self.started = 0
 
+    def begin(self):
+        self.started += 1
+        self.step()
+
     def step(self):
-        if self.started < len(self.groups) and self.level % self.spacing == 0:
+        if self.spacing and self.started < len(self.live) and self.level % self.spacing == 0:
             self.started += 1
         for group in self.live[: self.started]:
             for unit in list(group):
@@ -187,7 +190,7 @@
             self.step()
 
     def drain(self):
-        for group in range(len(self.groups)):
+        for group in range(len(self.live)):
             self.until(group)
 
 
@@ -199,11 +202,16 @@
         copy = pltpu.make_async_copy(src, dst, self.sems.at[len(self.made)])
         copy.start()
         self.made.append(copy)
-        return copy
+        return len(self.made) - 1
+
+    def wait(self, *which):
+        for at in which:
+            if self.made[at] is not None:
+                self.made[at].wait()
+                self.made[at] = None
 
     def finish(self):
-        for copy in self.made:
-            copy.wait()
+        self.wait(*range(len(self.made)))
 
 
 def gather_groups(place, sizes, own, whole, copies, local, orders):
@@ -265,7 +273,7 @@
         hxc.wait_recv()
 
     groups[0].append(rows_unit())
-    Levels(groups).drain()
+    Levels(groups, 3).drain()
     copies.finish()
 
 
@@ -314,29 +322,67 @@
         body(pl.ds(pl.multiple_of(i * tile, tile), tile))
 
 
-def forward_kernel(sizes, window, *refs):
+def exchange_rows(place, copies, n, sent, landed, make):
+    @pl.loop(0, n // LANES)
+    def _(i):
+        tile = pl.ds(pl.multiple_of(i * LANES, LANES), LANES)
+        theirs = pl.ds(pl.multiple_of((1 - place.c) * n + i * LANES, LANES), LANES)
+        sent[tile] = make(theirs).astype(low_type)
+
+    return copies.start(place, sent, landed, "c")
+
+
+def own_tiles(place, n, body):
+    @pl.loop(0, n // LANES)
+    def _(i):
+        tile = pl.ds(pl.multiple_of(i * LANES, LANES), LANES)
+        body(tile, pl.ds(pl.multiple_of(place.c * n + i * LANES, LANES), LANES))
+
+
+def blocks_of(place, rows_count, pair_count, span):
+    def at(block):
+        rows = pl.ds(pl.multiple_of(block * BLOCK, BLOCK), BLOCK)
+        if span == pair_count:
+            return rows, 0
+        ends = (place.x * (rows_count // BLOCK) + block + 1) * BLOCK
+        return rows, pl.multiple_of(jnp.maximum(ends - span, 0), BLOCK)
+
+    return at
+
+
+def forward_kernel(sizes, window, n_out, *refs):
     n_weights = len(sizes[2])
-    (
-        q_one, pair_one, out_w, lows, highs, enc_highs, gains, biases, residual, g_own, enc_own,
-        *own,
-    ) = refs[: 11 + n_weights]
-    outs = refs[11 + n_weights : 24 + 2 * n_weights]
-    whole = outs[:n_weights]
+    (lows, highs, enc_highs, gains, biases, *hbm) = refs[: 9 + 2 + 2 + n_weights - 2]
+    (q_in, pair_in, out_w_in, residual_in, g_own, enc_own, *own) = hbm
+    at = 11 + n_weights
+    outs, held = refs[at : at + n_out], refs[at + n_out : at + 2 * n_out]
+    (q_one, pair_one, out_w, residual, sent, landed, send_sems, recv_sems, local_sems) = refs[
+        at + 2 * n_out :
+    ]
+    whole = held[:n_weights]
     (
         g_all, enc_all, context_one, lse_one, residual_one, rows_two, q_two, pair_two, context_two,
-        lse_two, residual_two, rows_three, inner_pre,
-    ) = outs[n_weights:]
-    sent, landed, send_sems, recv_sems, local_sems = refs[24 + 2 * n_weights :]
+        lse_two, residual_two, rows_three, active, slope,
+    ) = held[n_weights:]
     query_w, pair_w, back_w, up_w, _ = whole
     place = Place()
-    greet(place, ("x", "y", "c", "down", "up"))
     copies = Copies(send_sems, recv_sems)
     local = Locals(local_sems)
+    loads = [
+        local.start(src, dst)
+        for src, dst in (
+            (q_in, q_one), (pair_in, pair_one), (out_w_in, out_w), (residual_in, residual),
+        )
+    ]
+    greet(place, ("x", "y", "c", "down", "up"))
     x, c = place.x, place.c
     n, e = residual.shape[0], enc_own.shape[0]
     heads_width = q_one.shape[1]
     mine = pl.ds(pl.multiple_of(c * n, 16), n)
-    others = pl.ds(pl.multiple_of((1 - c) * n, 16), n)
+
+    def flush(*names):
+        for ref in names:
+            local.start(ref, outs[[h is ref for h in held].index(True)])
 
     def e_at(xx, cc):
         return enc_all.at[pl.ds(pl.multiple_of((xx * 2 + cc) * e, 16), e)]
@@ -344,11 +390,12 @@
     ex = copies.start(place, enc_own, e_at(x, c), "x")
     ec = copies.start(place, enc_own, e_at(x, c), "c")
     gc = copies.start(place, g_own, g_all.at[mine], "c")
+    first = len(local.made)
     local.start(g_own, g_all.at[mine])
     local.start(enc_own, e_at(x, c))
     orders = ("xzy", "yzx", "xzy", "zxy") + GATHER_ORDERS * 2
     groups = gather_groups(place, sizes, own, whole, copies, local, orders)
-    local.finish()
+    local.wait(*range(first, len(local.made)))
 
     def enc_unit():
         yield
@@ -362,10 +409,10 @@
         exc.wait_recv()
 
     groups[0].append(enc_unit())
-    comm = Levels(groups)
+    comm = Levels(groups, 3)
 
     def attention(q_ref, pair_ref, low_of, high_of, o_ref, lse_ref, span):
-        keys_count = pair_ref.shape[0]
+        block_at = blocks_of(place, q_ref.shape[0], pair_ref.shape[0], span)
         for pair in range(heads_width // PAIR):
             comm.step()
             lanes = pl.ds(pair * PAIR, PAIR)
@@ -373,12 +420,7 @@
 
             @pl.loop(0, q_ref.shape[0] // BLOCK)
             def _(block):
-                rows = pl.ds(pl.multiple_of(block * BLOCK, BLOCK), BLOCK)
-                if span == keys_count:
-                    start = 0
-                else:
-                    ends = (x * (q_ref.shape[0] // BLOCK) + block + 1) * BLOCK
-                    start = pl.multiple_of(jnp.maximum(ends - span, 0), BLOCK)
+                rows, start = block_at(block)
                 here = pl.ds(start, span)
                 o_ref[rows, lanes], lse_ref[pair, block] = attend_step(
                     q_ref[rows, lanes],
@@ -390,57 +432,82 @@
                 )
 
     def branch(at, context, weight, before, after, gain_at, rows_ref):
-        @pl.loop(0, n // LANES)
-        def _(i):
-            tile = pl.ds(pl.multiple_of(i * LANES, LANES), LANES)
-            theirs = pl.ds(pl.multiple_of((1 - c) * n + i * LANES, LANES), LANES)
-            sent[at, tile] = outer_cols(context[theirs], weight[...]).astype(low_type)
-
-        over = copies.start(place, sent.at[at], landed.at[at], "c")
-
-        @pl.loop(0, n // LANES)
-        def _(i):
-            tile = pl.ds(pl.multiple_of(i * LANES, LANES), LANES)
-            own_rows = pl.ds(pl.multiple_of(c * n + i * LANES, LANES), LANES)
-            after[tile] = before[tile] + outer_cols(context[own_rows], weight[...])
-
+        over = exchange_rows(
+            place, copies, n, sent.at[at], landed.at[at],
+            lambda rows: outer_cols(context[rows], weight[...]),
+        )
+
+        def own_part(tile, rows):
+            after[tile] = before[tile] + outer_cols(context[rows], weight[...])
+
+        own_tiles(place, n, own_part)
         over.wait_recv()
 
-        @pl.loop(0, n // LANES)
-        def _(i):
-            tile = pl.ds(pl.multiple_of(i * LANES, LANES), LANES)
-            own_rows = pl.ds(pl.multiple_of(c * n + i * LANES, LANES), LANES)
+        def rest(tile, rows):
             total = after[tile] + landed[at, tile].astype(f32)
             after[tile] = total
-            rows_ref[own_rows] = norm_rows(
+            rows_ref[rows] = norm_rows(
                 total, gains[gain_at : gain_at + 1], biases[gain_at : gain_at + 1]
             ).astype(low_type)
 
+        own_tiles(place, n, rest)
         return copies.start(place, rows_ref.at[mine], rows_ref.at[mine], "c")
 
-    attention(q_one, pair_one, lambda r: lows[:, r], lambda r: highs[:, r], context_one, lse_one, window)
+    local.wait(*loads)
+    attention(
+        q_one, pair_one, lambda r: lows[:, r], lambda r: highs[:, r], context_one, lse_one, window
+    )
     comm.step()
     over = branch(0, context_one, out_w, residual, residual_one, 1, rows_two)
+    flush(context_one, lse_one, residual_one)
     comm.until(0)
-    loop_rows(enc_all.shape[0], BLOCK, lambda r: store(pair_two, r, matmul(enc_all[r], pair_w[...])))
+    loop_rows(
+        enc_all.shape[0], BLOCK, lambda r: store(pair_two, r, matmul(enc_all[r], pair_w[...]))
+    )
+    flush(query_w, pair_w, back_w, g_all, enc_all, pair_two)
     over.wait_recv()
     comm.step()
     loop_rows(2 * n, BLOCK, lambda r: store(q_two, r, matmul(rows_two[r], query_w[...])))
+    flush(rows_two, q_two)
     attention(
         q_two, pair_two, lambda r: jnp.zeros((1, BLOCK), jnp.int32), lambda r: enc_highs[:, r],
         context_two, lse_two, enc_all.shape[0],
     )
     comm.step()
     over = branch(1, context_two, back_w, residual_one, residual_two, 2, rows_three)
+    flush(context_two, lse_two, residual_two)
     comm.until(1)
     over.wait_recv()
-    loop_rows(2 * n, LANES, lambda r: store(inner_pre, r, matmul(rows_three[r], up_w[...])))
+    flush(rows_three, up_w)
+
+    def up(rows):
+        inner = matmul(rows_three[rows], up_w[...])
+        gate = 1.0 / (1.0 + jnp.exp(-inner))
+        active[rows] = (inner * gate).astype(low_type)
+        slope[rows] = (gate * (1.0 + inner * (1.0 - gate))).astype(low_type)
+
+    loop_rows(2 * n, LANES, up)
+    flush(active, slope)
     comm.drain()
+    flush(whole[-1])
+    local.finish()
     copies.finish()
 
 
 def store(ref, rows, values_in):
     ref[rows] = values_in.astype(ref.dtype)
+
+
+def low(*shape):
+    return jax.ShapeDtypeStruct(shape, low_type)
+
+
+def wide(*shape):
+    return jax.ShapeDtypeStruct(shape, f32)
+
+
+def scratch_like(shapes):
+    return [pltpu.VMEM(s.shape, s.dtype) for s in shapes]
 
 
 def forward(q_one, pair_one, out_w, lows, highs, enc_highs, gains, biases, residual, g_own, enc_own, shards, window):
@@ -451,34 +518,32 @@
     heads_width = q_one.shape[1]
     n_units = sum(sizes[2])
     n_copies = 8 + n_units * 11
-    lse = jax.ShapeDtypeStruct((heads_width // PAIR, 2 * n // BLOCK, 1, 2 * BLOCK), f32)
-
-    def low(*shape):
-        return jax.ShapeDtypeStruct(shape, low_type)
-
-    keep = jax.ShapeDtypeStruct((n, width), f32)
+    lse = wide(heads_width // PAIR, 2 * n // BLOCK, 1, 2 * BLOCK)
     out_shape = shapes + [
-        low(2 * n, width), low(4 * e, width), low(2 * n, heads_width), lse, keep, low(2 * n, width),
-        low(2 * n, heads_width), low(4 * e, 2 * heads_width), low(2 * n, heads_width), lse, keep,
-        low(2 * n, width), jax.ShapeDtypeStruct((2 * n, hidden), f32),
+        low(2 * n, width), low(4 * e, width), low(2 * n, heads_width), lse, wide(n, width), low(2 * n, width),
+        low(2 * n, heads_width), low(4 * e, 2 * heads_width), low(2 * n, heads_width), lse, wide(n, width),
+        low(2 * n, width), low(2 * n, hidden), low(2 * n, hidden),
     ]
     return pl.pallas_call(
-        functools.partial(forward_kernel, sizes, window),
+        functools.partial(forward_kernel, sizes, window, len(out_shape)),
         out_shape=out_shape,
-        in_specs=[VMEM_SPEC] * 9 + [ANY_SPEC] * (2 + len(shards)),
-        out_specs=[VMEM_SPEC] * len(out_shape),
-        scratch_shapes=[
-            pltpu.VMEM((2, n, width), low_type),
-            pltpu.VMEM((2, n, width), low_type),
+        in_specs=[VMEM_SPEC] * 5 + [ANY_SPEC] * (6 + len(shards)),
+        out_specs=[ANY_SPEC] * len(out_shape),
+        scratch_shapes=scratch_like(out_shape)
+        + scratch_like([q_one, pair_one, out_w, residual])
+        + scratch_like([low(2, n, width)] * 2)
+        + [
             pltpu.SemaphoreType.DMA((n_copies,)),
             pltpu.SemaphoreType.DMA((n_copies,)),
-            pltpu.SemaphoreType.DMA((2 + n_units,)),
+            pltpu.SemaphoreType.DMA((6 + n_units + len(out_shape),)),
         ],
         compiler_params=pltpu.CompilerParams(
             collective_id=2, has_side_effects=True, vmem_limit_bytes=60 * MIB
         ),
         name="forward",
-    )(q_one, pair_one, out_w, lows, highs, enc_highs, gains, biases, residual, g_own, enc_own, *shards)
+    )(
+        lows, highs, enc_highs, gains, biases, q_one, pair_one, out_w, residual, g_own, enc_own, *shards
+    )
 
 
 REDUCE_ORDERS = ("xyz", "xzy", "yxz", "yzx")
@@ -585,79 +650,402 @@
         out[...] = at(0, y, x)[...].astype(f32) + land[...].astype(f32)
 
 
-def reduce_kernel(sizes, *refs):
-    rows, cols, units_of = sizes
-    n_weights = len(units_of)
-    small = refs[0]
-    parts = refs[1 : 1 + n_weights]
-    outs = refs[1 + n_weights :]
-    small_out = outs[0]
-    sums = outs[1 : 1 + n_weights]
-    recv, small_recv, send_sems, recv_sems = outs[1 + n_weights :]
+def reduce_groups(place, rows, cols, part, recv, outs, copies, first):
+    return [
+        reduce_unit(
+            order, place, part, unit * 2 * cols, rows, cols, recv.at[first + unit], outs[unit], copies
+        )
+        for unit, order in enumerate(REDUCE_ORDERS)
+    ]
+
+
+def attention_back(place, comm, q_ref, pair_ref, low_of, high_of, o_ref, do_ref, lse_ref, span, dk_sum, dv_sum):
+    heads_width = q_ref.shape[1]
+    block_at = blocks_of(place, q_ref.shape[0], pair_ref.shape[0], span)
+    for pair in range(heads_width // PAIR):
+        comm.step()
+        lanes = pl.ds(pair * PAIR, PAIR)
+        value_lanes = pl.ds(heads_width + pair * PAIR, PAIR)
+        dk_sum[...] = jnp.zeros_like(dk_sum)
+        dv_sum[...] = jnp.zeros_like(dv_sum)
+
+        @pl.loop(0, q_ref.shape[0] // BLOCK)
+        def _(block):
+            rows, start = block_at(block)
+            here = pl.ds(start, span)
+            dq, dk, dv = attend_back_step(
+                q_ref[rows, lanes],
+                pair_ref[here, lanes],
+                pair_ref[here, value_lanes],
+                low_of(rows),
+                high_of(rows),
+                start,
+                o_ref[rows, lanes],
+                do_ref[rows, lanes],
+                lse_ref[pair, block],
+            )
+            q_ref[rows, lanes] = dq
+            dk_sum[here] += dk
+            dv_sum[here] += dv
+
+        pair_ref[:, lanes] = dk_sum[...].astype(low_type)
+        pair_ref[:, value_lanes] = dv_sum[...].astype(low_type)
+
+
+def loop_cols(count, tile, body):
+    loop_rows(count, tile, body)
+
+
+def norm_back_tile(small, at, incoming, before, gain_row):
+    _, unit_rows, inverse = norm_forward(before, jnp.ones_like(gain_row), jnp.zeros_like(gain_row))
+    result, gain_sum, bias_sum = norm_backward(incoming, unit_rows, inverse, gain_row)
+    small[at : at + 1] += gain_sum[None]
+    small[at + 3 : at + 4] += bias_sum[None]
+    return result
+
+
+def back_one_kernel(sizes, *refs):
+    rows, cols = sizes
+    (
+        enc_highs, gains, lse_two,
+        down_in, up_in, active_in, slope_in, g_in, rows_in, residual_in, q_in, pair_in, context_in, back_in,
+        down_sum, up_sum, small, out_tokens, grad_out, back_out, dq_out, dpair_out,
+        down_w, up_w, active, slope, g_all, rows_three, residual, q_two, pair_two, context, back_w,
+        part_down, part_up, recv, sent, landed, grad, g_two, back_part, grad_context, tokens_out, dk_sum, dv_sum,
+        send_sems, recv_sems, local_sems,
+    ) = refs
     place = Place()
+    copies = Copies(send_sems, recv_sems)
+    local = Locals(local_sems)
+    c = place.c
+    g_at, active_at, down_at, slope_at, rows_at, up_at, res_at, con_at, back_at, q_at, pair_at = [
+        local.start(src, dst)
+        for src, dst in (
+            (g_in, g_all), (active_in, active), (down_in, down_w), (slope_in, slope), (rows_in, rows_three),
+            (up_in, up_w), (residual_in, residual), (context_in, context), (back_in, back_w),
+            (q_in, q_two), (pair_in, pair_two),
+        )
+    ]
+    greet(place, ("x", "y", "c", "down", "up"))
+    n, width = residual.shape
+    mine = pl.ds(pl.multiple_of(c * n, 16), n)
+    comm = Levels(
+        [
+            reduce_groups(place, rows, cols, part_down, recv, [down_sum.at[k] for k in range(4)], copies, 0),
+            reduce_groups(place, rows, cols, part_up, recv, [up_sum.at[k] for k in range(4)], copies, 4),
+        ]
+    )
+    small[...] = jnp.zeros_like(small)
+    local.wait(g_at, active_at)
+    loop_cols(width, BLOCK, lambda t: store(part_down, t, inner_rows(g_all[:, t], active[...])))
+    comm.begin()
+    local.wait(down_at, slope_at)
+
+    def inner(tile):
+        slope[tile] = (matmul(g_all[tile], down_w[...]) * slope[tile].astype(f32)).astype(low_type)
+
+    loop_rows(2 * n, LANES, inner)
+    local.wait(rows_at)
+    loop_cols(width, BLOCK, lambda t: store(part_up, t, inner_rows(rows_three[:, t], slope[...])))
+    comm.begin()
+    local.wait(up_at)
+    over = exchange_rows(
+        place, copies, n, sent.at[0], landed.at[0], lambda r: outer_cols(slope[r], up_w[...])
+    )
+
+    def own_part(tile, rows_here):
+        grad[tile] = outer_cols(slope[rows_here], up_w[...])
+
+    own_tiles(place, n, own_part)
+    comm.step()
+    out_over = exchange_rows(
+        place, copies, n, sent.at[1], landed.at[1], lambda r: outer_cols(active[r], down_w[...])
+    )
+    local.wait(res_at)
+    over.wait_recv()
+
+    def norm_part(tile, rows_here):
+        incoming = grad[tile] + landed[0, tile].astype(f32)
+        total = g_all[rows_here].astype(f32) + norm_back_tile(
+            small, 2, incoming, residual[tile], gains[2:3]
+        )
+        grad[tile] = total
+        g_two[rows_here] = total.astype(low_type)
+
+    own_tiles(place, n, norm_part)
+    g_over = copies.start(place, g_two.at[mine], g_two.at[mine], "c")
+    local.start(grad, grad_out)
+    comm.step()
+    out_over.wait_recv()
+
+    def out_part(tile, rows_here):
+        total = residual[tile] + outer_cols(active[rows_here], down_w[...])
+        tokens_out[tile] = (total + landed[1, tile].astype(f32)).astype(low_type)
+
+    own_tiles(place, n, out_part)
+    local.start(tokens_out, out_tokens)
+    local.wait(con_at, back_at)
+    g_over.wait_recv()
+    loop_rows(2 * n, BLOCK, lambda r: store(grad_context, r, matmul(g_two[r], back_w[...])))
+    loop_cols(width, BLOCK, lambda t: store(back_part, t, inner_rows(g_two[:, t], context[...])))
+    local.start(back_part, back_out)
+    local.wait(q_at, pair_at)
+    attention_back(
+        place, comm, q_two, pair_two, lambda r: jnp.zeros((1, BLOCK), jnp.int32),
+        lambda r: enc_highs[:, r], context, grad_context, lse_two, pair_two.shape[0], dk_sum, dv_sum,
+    )
+    local.start(q_two, dq_out)
+    local.start(pair_two, dpair_out)
+    comm.drain()
+    local.finish()
+    copies.finish()
+
+
+def back_one(enc_highs, gains, lse_two, down_w, up_w, active, slope, g_all, rows_three, residual, q_two, pair_two, context, back_w, rows, cols):
+    n, width = residual.shape
+    heads_width = q_two.shape[1]
+    unit_sum = wide(4, rows, cols)
+    hbm = [down_w, up_w, active, slope, g_all, rows_three, residual, q_two, pair_two, context, back_w]
+    out_shape = [
+        unit_sum, unit_sum, wide(8, width), low(n, width), wide(n, width), low(width, heads_width),
+        low(2 * n, heads_width), low(*pair_two.shape),
+    ]
+    n_copies = 8 * 15 + 3
+    return pl.pallas_call(
+        functools.partial(back_one_kernel, (rows, cols)),
+        out_shape=out_shape,
+        in_specs=[VMEM_SPEC] * 3 + [ANY_SPEC] * len(hbm),
+        out_specs=[VMEM_SPEC] * 3 + [ANY_SPEC] * 5,
+        scratch_shapes=scratch_like(hbm)
+        + scratch_like(
+            [
+                low(*down_w.shape), low(*up_w.shape), low(8, rows * 15, cols), low(2, n, width),
+                low(2, n, width), wide(n, width), low(2 * n, width), low(width, heads_width),
+                low(2 * n, heads_width), low(n, width), wide(pair_two.shape[0], PAIR), wide(pair_two.shape[0], PAIR),
+            ]
+        )
+        + [
+            pltpu.SemaphoreType.DMA((n_copies,)),
+            pltpu.SemaphoreType.DMA((n_copies,)),
+            pltpu.SemaphoreType.DMA((len(hbm) + 5,)),
+        ],
+        compiler_params=pltpu.CompilerParams(
+            collective_id=1, has_side_effects=True, vmem_limit_bytes=60 * MIB
+        ),
+        name="back_one",
+    )(enc_highs, gains, lse_two, *hbm)
+
+
+def back_two_kernel(sizes, window, *refs):
+    rows, cols = sizes
+    (
+        lows, highs, gains, lse_one, small_in,
+        dq_in, dpair_in, rows_two_in, enc_in, query_in, pair_w_in, back_in, grad_in, residual_in, context_in,
+        out_w_in, q_in, pair_in, rows_one_in, qkv_in, tokens_in,
+        back_sum, query_sum, pair_sum, out_sum, qkv_sum, small_out, in_grad, enc_grad,
+        dq_two, dpair_two, rows_two, enc_all, query_w, pair_w, grad, residual, context, out_w, q_one,
+        pair_one, rows_one, qkv_w, tokens,
+        part_cross, part_self, recv, sent, landed, total, g_one, grad_context, dk_sum, dv_sum,
+        enc_sent, enc_landed, enc_total, small_recv, send_sems, recv_sems, local_sems,
+    ) = refs
+    place = Place()
+    copies = Copies(send_sems, recv_sems)
+    local = Locals(local_sems)
+    x, c = place.x, place.c
+    n, width = residual.shape
+    heads_width = q_one.shape[1]
+    e = enc_grad.shape[0]
+    (
+        dpair_at, enc_at, dq_at, rows_two_at, back_at, query_at, pair_w_at, grad_at, res_at, con_at, out_w_at,
+        q_at, pair_at, rows_one_at, qkv_at, tokens_at,
+    ) = [
+        local.start(src, dst)
+        for src, dst in (
+            (dpair_in, dpair_two), (enc_in, enc_all), (dq_in, dq_two), (rows_two_in, rows_two),
+            (back_in, part_cross.at[:, pl.ds(0, heads_width)]), (query_in, query_w), (pair_w_in, pair_w),
+            (grad_in, grad), (residual_in, residual), (context_in, context), (out_w_in, out_w), (q_in, q_one),
+            (pair_in, pair_one), (rows_one_in, rows_one), (qkv_in, qkv_w), (tokens_in, tokens),
+        )
+    ]
     greet(place, ("x", "y", "c", "down", "up", "z2"))
-    copies = Copies(send_sems, recv_sems)
-    groups, group = [], []
-    index = 0
-    for which, count in enumerate(units_of):
-        for unit in range(count):
-            order = REDUCE_ORDERS[len(group)]
-            group.append(
-                reduce_unit(
-                    order,
-                    place,
-                    parts[which],
-                    unit * 2 * cols,
-                    rows,
-                    cols,
-                    recv.at[index],
-                    sums[which].at[unit],
-                    copies,
-                )
-            )
-            index += 1
-            if len(group) == len(REDUCE_ORDERS):
-                groups.append(group)
-                group = []
+    mine = pl.ds(pl.multiple_of(c * n, 16), n)
 
     def small_unit():
-        small_out[0] = small[...]
         for at, which in enumerate(("c", "x", "y", "z1", "z2")):
             copy = copies.start(place, small_out.at[at], small_recv.at[at], which)
             yield
             copy.wait_recv()
             small_out[at + 1] = small_out[at] + small_recv[at]
 
-    groups[0].append(small_unit())
-    Levels(groups).drain()
+    cross_sums = [back_sum.at[0], query_sum.at[0], pair_sum.at[0], pair_sum.at[1]]
+    self_sums = [out_sum.at[0], qkv_sum.at[0], qkv_sum.at[1], qkv_sum.at[2]]
+    comm = Levels(
+        [
+            reduce_groups(place, rows, cols, part_cross, recv, cross_sums, copies, 0),
+            reduce_groups(place, rows, cols, part_self, recv, self_sums, copies, 4),
+            [small_unit()],
+        ]
+    )
+    small = small_out.at[0]
+    small[...] = small_in[...]
+    second = pl.ds(heads_width, heads_width)
+    rest = pl.ds(2 * heads_width, 2 * heads_width)
+    local.wait(dpair_at, enc_at)
+
+    def pair_grads(t):
+        part_cross[t, rest] = inner_rows(enc_all[:, t], dpair_two[...]).astype(low_type)
+
+    loop_cols(width, BLOCK, pair_grads)
+    local.wait(dq_at, rows_two_at, back_at)
+
+    def query_grads(t):
+        part_cross[t, second] = inner_rows(rows_two[:, t], dq_two[...]).astype(low_type)
+
+    loop_cols(width, BLOCK, query_grads)
+    comm.begin()
+    local.wait(query_at)
+    over = exchange_rows(
+        place, copies, n, sent.at[0], landed.at[0], lambda r: outer_cols(dq_two[r], query_w[...])
+    )
+
+    def own_part(tile, rows_here):
+        total[tile] = outer_cols(dq_two[rows_here], query_w[...])
+
+    own_tiles(place, n, own_part)
+    local.wait(pair_w_at)
+
+    def enc_rows(xx, cc):
+        return pl.ds(pl.multiple_of((xx * 2 + cc) * e, LANES), e)
+
+    def enc_term(xx, cc):
+        return outer_cols(dpair_two[enc_rows(xx, cc)], pair_w[...])
+
+    enc_sent[0] = enc_term(x, 1 - c).astype(low_type)
+    enc_sent[1] = enc_term(1 - x, 1 - c).astype(low_type)
+    enc_over = copies.start(place, enc_sent.at[pl.ds(0, 2)], enc_landed.at[pl.ds(0, 2)], "c")
+    local.wait(grad_at, res_at)
+    over.wait_recv()
+
+    def norm_part(tile, rows_here):
+        incoming = total[tile] + landed[0, tile].astype(f32)
+        after = grad[tile] + norm_back_tile(small, 1, incoming, residual[tile], gains[1:2])
+        grad[tile] = after
+        g_one[rows_here] = after.astype(low_type)
+
+    own_tiles(place, n, norm_part)
+    g_over = copies.start(place, g_one.at[mine], g_one.at[mine], "c")
+    comm.step()
+    enc_over.wait_recv()
+    enc_sent[2] = (enc_term(1 - x, c) + enc_landed[1].astype(f32)).astype(low_type)
+    enc_far = copies.start(place, enc_sent.at[2], enc_landed.at[2], "x")
+    enc_total[...] = enc_term(x, c) + enc_landed[0].astype(f32)
+    local.wait(con_at, out_w_at)
+    g_over.wait_recv()
+    loop_rows(2 * n, BLOCK, lambda r: store(grad_context, r, matmul(g_one[r], out_w[...])))
+
+    def out_grads(t):
+        part_self[t, pl.ds(0, heads_width)] = inner_rows(g_one[:, t], context[...]).astype(low_type)
+
+    loop_cols(width, BLOCK, out_grads)
+    local.wait(q_at, pair_at)
+    attention_back(
+        place, comm, q_one, pair_one, lambda r: lows[:, r], lambda r: highs[:, r],
+        context, grad_context, lse_one, window, dk_sum, dv_sum,
+    )
+    local.wait(rows_one_at)
+    chip_rows = pl.ds(pl.multiple_of(x * 2 * n, LANES), 2 * n)
+
+    def self_grads(t):
+        part_self[t, second] = inner_rows(rows_one[chip_rows, t], q_one[...]).astype(low_type)
+        part_self[t, rest] = inner_rows(rows_one[:, t], pair_one[...]).astype(low_type)
+
+    loop_cols(width, BLOCK, self_grads)
+    comm.begin()
+    enc_far.wait_recv()
+    enc_total[...] += enc_landed[2].astype(f32)
+    local.start(enc_total, enc_grad)
+    local.wait(qkv_at)
+    q_lanes, kv_lanes = pl.ds(0, heads_width), pl.ds(heads_width, 2 * heads_width)
+
+    def key_term(xx, local_rows):
+        at = pl.ds(pl.multiple_of(xx * 2 * n + local_rows.start, LANES), local_rows.size)
+        return outer_cols(pair_one[at], qkv_w[:, kv_lanes])
+
+    def query_term(local_rows):
+        return outer_cols(q_one[local_rows], qkv_w[:, q_lanes])
+
+    far_over = exchange_rows(
+        place, copies, n, sent.at[1], landed.at[1], lambda r: key_term(1 - x, r)
+    )
+    near_over = exchange_rows(
+        place, copies, n, sent.at[2], landed.at[2], lambda r: key_term(x, r) + query_term(r)
+    )
+    far_over.wait_recv()
+
+    def far_part(tile, rows_here):
+        sent[3, tile] = (key_term(1 - x, rows_here) + landed[1, tile].astype(f32)).astype(low_type)
+
+    own_tiles(place, n, far_part)
+    chip_over = copies.start(place, sent.at[3], landed.at[3], "x")
+
+    def near_part(tile, rows_here):
+        total[tile] = key_term(x, rows_here) + query_term(rows_here)
+
+    own_tiles(place, n, near_part)
+    comm.step()
+    local.wait(tokens_at)
+    near_over.wait_recv()
+    chip_over.wait_recv()
+
+    def last_part(tile, rows_here):
+        incoming = total[tile] + landed[2, tile].astype(f32) + landed[3, tile].astype(f32)
+        grad[tile] += norm_back_tile(small, 0, incoming, tokens[tile].astype(f32), gains[0:1])
+
+    own_tiles(place, n, last_part)
+    local.start(grad, in_grad)
+    comm.begin()
+    comm.drain()
+    local.finish()
     copies.finish()
 
 
-def reduce_grads(small, parts, rows, cols):
-    units_of = tuple(p.shape[1] // (2 * cols) for p in parts)
-    n_units = sum(units_of)
-    vmem = pl.BlockSpec(memory_space=pltpu.VMEM)
-    out_shape = [jax.ShapeDtypeStruct((6,) + small.shape, f32)] + [
-        jax.ShapeDtypeStruct((k, rows, cols), f32) for k in units_of
+def back_two(lows, highs, gains, lse_one, small, hbm, rows, cols, window, enc_rows):
+    grad, q_one, pair_one = hbm[7], hbm[11], hbm[12]
+    n, width = grad.shape
+    heads_width = q_one.shape[1]
+
+    def sums(k):
+        return wide(k, rows, cols)
+
+    out_shape = [
+        sums(1), sums(1), sums(2), sums(1), sums(3), wide(6, 8, width), wide(n, width), wide(enc_rows, width),
     ]
-    n_copies = 5 + n_units * 15
+    n_copies = 8 * 15 + 8 + 5
+    held = hbm[:6] + hbm[7:]
     return pl.pallas_call(
-        functools.partial(reduce_kernel, (rows, cols, units_of)),
+        functools.partial(back_two_kernel, (rows, cols), window),
         out_shape=out_shape,
-        in_specs=[vmem] * (1 + len(parts)),
-        out_specs=[vmem] * len(out_shape),
-        scratch_shapes=[
-            pltpu.VMEM((n_units, rows * 15, cols), low_type),
-            pltpu.VMEM((5,) + small.shape, f32),
+        in_specs=[VMEM_SPEC] * 5 + [ANY_SPEC] * len(hbm),
+        out_specs=[VMEM_SPEC] * 6 + [ANY_SPEC] * 2,
+        scratch_shapes=scratch_like(held)
+        + scratch_like(
+            [
+                low(width, 4 * heads_width), low(width, 4 * heads_width), low(8, rows * 15, cols),
+                low(4, n, width), low(4, n, width), wide(n, width), low(2 * n, width),
+                low(2 * n, heads_width), wide(pair_one.shape[0], PAIR), wide(pair_one.shape[0], PAIR),
+                low(3, enc_rows, width), low(3, enc_rows, width), wide(enc_rows, width), wide(5, 8, width),
+            ]
+        )
+        + [
             pltpu.SemaphoreType.DMA((n_copies,)),
             pltpu.SemaphoreType.DMA((n_copies,)),
+            pltpu.SemaphoreType.DMA((len(hbm) + 2,)),
         ],
-        input_output_aliases={},
         compiler_params=pltpu.CompilerParams(
-            collective_id=1, has_side_effects=True, vmem_limit_bytes=52 * MIB
+            collective_id=3, has_side_effects=True, vmem_limit_bytes=62 * MIB
         ),
-        name="reduce_grads",
-    )(small, *parts)
+        name="back_two",
+    )(lows, highs, gains, lse_one, small, *hbm)
 
 
 BLOCK = 256
@@ -669,13 +1057,6 @@
     return jnp.concatenate(
         [jnp.where(lane < HD, values_in, zero), jnp.where(lane >= HD, values_in, zero)], axis=0
     )
-
-
-def window_start(place_ref, window, keys):
-    if window == keys:
-        return 0
-    ends = (place_ref[0] + pl.program_id(1) + 1) * BLOCK
-    return pl.multiple_of(jnp.maximum(ends - window, 0), BLOCK)
 
 
 def key_scores(queries, keys, lows, highs, start):
@@ -698,44 +1079,14 @@
     return pair.T.astype(low_type), peak + jnp.log(total)
 
 
-def attention_specs(rows, keys):
-    def block(i, j, p):
-        return (j, i)
-
-    def whole(i, j, p):
-        return (0, i)
-
-    def line(i, j, p):
-        return (0, j)
-
-    q_spec = pl.BlockSpec((BLOCK, PAIR), block)
-    k_spec = pl.BlockSpec((keys, PAIR), whole)
-    l_spec = pl.BlockSpec((1, BLOCK), line)
-    lse_spec = pl.BlockSpec((1, 1, 1, 2 * BLOCK), lambda i, j, p: (i, j, 0, 0))
-    return q_spec, k_spec, l_spec, lse_spec
-
-
-def attend_back_kernel(
-    window, place_ref, q_ref, k_ref, v_ref, low_ref, high_ref, o_ref, do_ref, lse_ref,
-    dq_ref, dk_ref, dv_ref, dk_sum, dv_sum,
-):
-    scale = jnp.asarray(HD**-0.5, low_type)
-    start = window_start(place_ref, window, k_ref.shape[0])
-    here = pl.ds(start, window)
-    rows = q_ref.shape[0]
-
-    @pl.when(pl.program_id(1) == 0)
-    def _():
-        dk_sum[...] = jnp.zeros_like(dk_sum)
-        dv_sum[...] = jnp.zeros_like(dv_sum)
-
-    keys, values = k_ref[here], v_ref[here]
-    queries = split_heads(q_ref[...] * scale)
-    grads = split_heads(do_ref[...])
-    scores = key_scores(queries, keys, low_ref[...], high_ref[...], start)
-    probs = jnp.exp(scores - lse_ref[0, 0])
+def attend_back_step(q_block, keys, values, lows, highs, start, context, grad_context, lse):
+    rows = q_block.shape[0]
+    queries = split_heads(q_block * jnp.asarray(HD**-0.5, low_type))
+    grads = split_heads(grad_context)
+    scores = key_scores(queries, keys, lows, highs, start)
+    probs = jnp.exp(scores - lse)
     grad_probs = outer_cols(values, grads)
-    product = (do_ref[...].astype(f32) * o_ref[...].astype(f32)).T
+    product = (grad_context.astype(f32) * context.astype(f32)).T
     inner = jnp.concatenate(
         [
             jnp.sum(product[:HD], axis=0, keepdims=True),
@@ -744,49 +1095,11 @@
         axis=1,
     )
     grad_scores = (probs * (grad_probs - inner)).astype(low_type)
-    dv_sum[here] += matmul(probs.astype(low_type), grads)
-    dk_sum[here] += matmul(grad_scores, queries)
+    dv = matmul(probs.astype(low_type), grads)
+    dk = matmul(grad_scores, queries)
     grad_queries = inner_rows(keys, grad_scores) * HD**-0.5
     pair = jnp.concatenate([grad_queries[:HD, :rows], grad_queries[HD:, rows:]], axis=0)
-    dq_ref[...] = pair.T.astype(low_type)
-
-    @pl.when(pl.program_id(1) == pl.num_programs(1) - 1)
-    def _():
-        dk_ref[...] = dk_sum[...].astype(low_type)
-        dv_ref[...] = dv_sum[...].astype(low_type)
-
-
-def attend_back(place, queries, keys, values, lows, highs, context, grads, lse, window):
-    rows, width = queries.shape
-    count = keys.shape[0]
-    pairs, blocks = width // PAIR, rows // BLOCK
-    q_spec, k_spec, l_spec, lse_spec = attention_specs(rows, count)
-    cost = pl.CostEstimate(
-        flops=20 * rows * window * width,
-        bytes_accessed=2 * width * (4 * rows + 4 * count),
-        transcendentals=rows * window * width // HD,
-    )
-    return pl.pallas_call(
-        functools.partial(attend_back_kernel, window),
-        out_shape=[
-            jax.ShapeDtypeStruct((rows, width), low_type),
-            jax.ShapeDtypeStruct((count, width), low_type),
-            jax.ShapeDtypeStruct((count, width), low_type),
-        ],
-        grid_spec=pltpu.PrefetchScalarGridSpec(
-            num_scalar_prefetch=1,
-            grid=(pairs, blocks),
-            in_specs=[q_spec, k_spec, k_spec, l_spec, l_spec, q_spec, q_spec, lse_spec],
-            out_specs=[q_spec, k_spec, k_spec],
-            scratch_shapes=[pltpu.VMEM((count, PAIR), f32), pltpu.VMEM((count, PAIR), f32)],
-        ),
-        compiler_params=pltpu.CompilerParams(vmem_limit_bytes=48 * MIB),
-        cost_estimate=cost,
-        name="attend_back",
-    )(place, queries, keys, values, lows, highs, context, grads, lse)
-
-
-SWAP = ((0, 1), (1, 0))
+    return pair.T.astype(low_type), dk, dv
 
 
 def width_orders(outer, width):
@@ -825,7 +1138,7 @@
     spread, gathered_back = width_orders(outer, tokens.shape[1])
     tokens, encoder, out_grad = spread(tokens), spread(encoder[0]), spread(out_grad)
     norm_gains, norm_biases = spread(norm_gains), spread(norm_biases)
-    core, chip = lax.axis_index("c"), lax.axis_index("x")
+    chip = lax.axis_index("x")
     own = tokens.shape[0]
     half = 2 * own
     segment = seg_ids[0]
@@ -851,31 +1164,16 @@
     rows = shards[0].shape[1]
 
     residual = tokens.astype(f32)
-    normed, unit_one, inverse_one = norm_forward(residual, norm_gains[0], norm_biases[0])
+    normed = norm_rows(residual, norm_gains[0], norm_biases[0])
     rows_one, qkv_w, out_w = gather_first(normed.astype(low_type), shards[:2])
 
     heads_width = 2 * cols
-
-    def half_of(values_in, which):
-        return lax.dynamic_slice_in_dim(values_in, which * own, own, 0)
-
-    def core_sum(partial):
-        theirs = lax.ppermute(half_of(partial, 1 - core).astype(low_type), "c", SWAP)
-        return half_of(partial, core) + theirs.astype(f32)
-
-    def core_rows(mine):
-        theirs = lax.ppermute(mine, "c", SWAP)
-        return jnp.concatenate(
-            [jnp.where(core == 0, mine, theirs), jnp.where(core == 0, theirs, mine)], axis=0
-        )
 
     first = chip * half
     here = lax.dynamic_slice_in_dim(segment, first, half, 0)
     lows = jnp.sum((segment[None, :] < here[:, None]).astype(jnp.int32), axis=1)[None]
     highs = (first + jnp.arange(half, dtype=jnp.int32))[None]
-    enc_lows = jnp.zeros_like(highs)
     enc_highs = jnp.broadcast_to(enc_lens[0] - 1, highs.shape)
-    place = (chip * (half // BLOCK))[None].astype(jnp.int32)
     window = min(seq_len, seq_len // 2 + BLOCK)
 
     chip_rows = lax.dynamic_slice_in_dim(rows_one, first, half, 0)
@@ -883,81 +1181,25 @@
     pair_one = matmul(rows_one, qkv_w[:, heads_width:]).astype(low_type)
     (
         query_w, pair_w, back_w, up_w, down_w, grads_three, enc_full, context_one, lse_one, residual_one,
-        rows_two, queries_two, pair_two, context_two, lse_two, residual_two, rows_three, inner_pre,
+        rows_two, queries_two, pair_two, context_two, lse_two, residual_two, rows_three, active, slope,
     ) = forward(
         queries_one, pair_one, out_w, lows, highs, enc_highs, norm_gains, norm_biases, residual,
         out_grad, encoder, shards[2:], window,
     )
-    enc_count = enc_full.shape[0]
-    keys_one, values_one = pair_one[:, :heads_width], pair_one[:, heads_width:]
-    keys_two, values_two = pair_two[:, :heads_width], pair_two[:, heads_width:]
-    unit_two, inverse_two = norm_forward(residual_one, norm_gains[1], norm_biases[1])[1:]
-    unit_three, inverse_three = norm_forward(residual_two, norm_gains[2], norm_biases[2])[1:]
-
-    sigmoid_pre = jax.nn.sigmoid(inner_pre)
-    active = (inner_pre * sigmoid_pre).astype(low_type)
-    out_tokens = (residual_two + core_sum(outer_cols(active, down_w))).astype(low_type)
-
-    grad_active = matmul(grads_three, down_w)
-    slope = sigmoid_pre * (1.0 + inner_pre * (1.0 - sigmoid_pre))
-    grad_inner = (grad_active * slope).astype(low_type)
-    down_grad = inner_rows(grads_three, active).astype(low_type)
-    up_grad = inner_rows(rows_three, grad_inner).astype(low_type)
-    grad_normed = core_sum(outer_cols(grad_inner, up_w))
-    grad_residual, gain_three, bias_three = norm_backward(
-        grad_normed, unit_three, inverse_three, norm_gains[2]
-    )
-    grad_total = out_grad.astype(f32) + grad_residual
-
-    grads_two = core_rows(grad_total.astype(low_type))
-    grad_context = matmul(grads_two, back_w).astype(low_type)
-    back_grad = inner_rows(grads_two, context_two).astype(low_type)
-    grad_queries, grad_keys, grad_values = attend_back(
-        place, queries_two, keys_two, values_two, enc_lows, enc_highs,
-        context_two, grad_context, lse_two, enc_count,
-    )
-    query_grad = inner_rows(rows_two, grad_queries).astype(low_type)
-    grad_pair = jnp.concatenate([grad_keys, grad_values], axis=1)
-    pair_grad = inner_rows(enc_full, grad_pair).astype(low_type)
-    enc_grad = lax.psum_scatter(
-        outer_cols(grad_pair, pair_w).astype(low_type), ("x", "c"), scatter_dimension=0, tiled=True
-    ).astype(f32)[None]
-    grad_normed = core_sum(outer_cols(grad_queries, query_w))
-    grad_residual, gain_two, bias_two = norm_backward(
-        grad_normed, unit_two, inverse_two, norm_gains[1]
-    )
-    grad_total = grad_total + grad_residual
-
-    grads_one = core_rows(grad_total.astype(low_type))
-    grad_context = matmul(grads_one, out_w).astype(low_type)
-    out_w_grad = inner_rows(grads_one, context_one).astype(low_type)
-    grad_queries, grad_keys, grad_values = attend_back(
-        place, queries_one, keys_one, values_one, lows, highs,
-        context_one, grad_context, lse_one, window,
-    )
-    grad_pair = jnp.concatenate([grad_keys, grad_values], axis=1)
-    qkv_grad = jnp.concatenate(
+    down_sum, up_sum, small, out_tokens, grad_two, back_grad, grad_queries, grad_pair = back_one(
+        enc_highs, norm_gains, lse_two, down_w, up_w, active, slope, grads_three, rows_three, residual_two,
+        queries_two, pair_two, context_two, back_w, rows, cols,
+    )
+    back_sum, query_sum, pair_sum, out_sum, qkv_sum, small, in_grad, enc_grad = back_two(
+        lows, highs, norm_gains, lse_one, small,
         [
-            inner_rows(chip_rows, grad_queries).astype(low_type),
-            inner_rows(rows_one, grad_pair).astype(low_type),
+            grad_queries, grad_pair, rows_two, enc_full, query_w, pair_w, back_grad, grad_two, residual_one,
+            context_one, out_w, queries_one, pair_one, rows_one, qkv_w, tokens,
         ],
-        axis=1,
-    )
-    key_term = outer_cols(grad_pair, qkv_w[:, heads_width:])
-    query_term = outer_cols(grad_queries, qkv_w[:, :heads_width])
-    mine = lax.dynamic_slice_in_dim(key_term, first, half, 0) + query_term
-    others = lax.dynamic_slice_in_dim(key_term, (1 - chip) * half, half, 0)
-    to_chip = lax.ppermute(core_sum(others).astype(low_type), "x", SWAP)
-    grad_normed = core_sum(mine) + to_chip.astype(f32)
-    grad_residual, gain_one, bias_one = norm_backward(
-        grad_normed, unit_one, inverse_one, norm_gains[0]
-    )
-    in_grad = grad_total + grad_residual
-
-    small = jnp.stack([gain_one, gain_two, gain_three, bias_one, bias_two, bias_three])
-    small = jnp.concatenate([small, jnp.zeros((2, width), f32)], axis=0)
-    grads = [up_grad, down_grad, back_grad, query_grad, pair_grad, out_w_grad, qkv_grad]
-    small, *sums = reduce_grads(small, grads, rows, cols)
+        rows, cols, window, encoder.shape[0],
+    )
+    enc_grad = enc_grad[None]
+    sums = [up_sum, down_sum, back_sum, query_sum, pair_sum, out_sum, qkv_sum]
     small = small[-1]
     if outer > 1:
         small = lax.psum(small, "o")

time: 580 us -> 454 us (0.78); the launches traced: 570 us -> 451 us
  matrix products: 64.7 us -> 7.16 us
  other arithmetic: 33.1 us -> 8.69 us
  local copies, waits for them, and re-layouts: 36.4 us -> 18.6 us
  between operations: 15.6 us -> 1.79 us
  waiting for transfers between devices: 13.7 us -> 0 us
  Pallas kernels: 403 us -> 415 us
    dot_general x14 -> x0, matrix products: 46.9 us -> none  [the longest x8 29 us: inner_rows(): lax.dot_general(left, right, (((0,), (0,)), ((), ())), preferred_element_...]
    ppermute x8 -> x0, waiting for transfers between devices: 13.7 us -> none  [the longest x1 13.7 us: on_device(): to_chip = lax.ppermute(core_sum(others).astype(low_type), 'x', SWAP)]
    pallas_call x4 -> x3, Pallas kernels: 342 us -> 353 us  [the longest x1 130 us: back_two(): pl.pallas_call(functools.partial(back_two_kernel, (rows, cols), window),...]
    dot_general x5 -> x2, matrix products: 17.8 us -> 7.16 us  [matmul(): return jnp.dot(left, right, preferred_element_type=f32)]
    convert_element_type x4 -> x0, other arithmetic: 9.82 us -> none  [the longest x1 4.6 us: on_device(): active = (inner_pre * sigmoid_pre).astype(low_type)]
    unnamed x111 -> x46, local copies, waits for them, and re-layouts: 18.6 us -> 12.3 us
    slice x5 -> x4, local copies, waits for them, and re-layouts: 5.83 us -> 0.01 us  [on_device(): normed = norm_rows(residual, norm_gains[0], norm_biases[0])]
  transfers between devices with their start and end apart: 9 -> 0, of which waited for: 1 -> 0; matrix products, arithmetic and copies ran while one was open for 13% -> 0% of each run, Pallas kernels for 32% -> 0%
where the time goes in v3:
time: 454 us; the launch traced here: 451 us
  Pallas kernels  415 us (91%)
  local copies, waits for them, and re-layouts  18.6 us (4%)
  other arithmetic  8.69 us (2%)
  matrix products  7.16 us (2%)
    pallas_call x1, Pallas kernels, back_two(): pl.pallas_call(functools.partial(back_two_kernel, (rows, cols), window),...  130 us
    pallas_call x1, Pallas kernels, forward(): pl.pallas_call(functools.partial(forward_kernel, sizes, window, len(out_s...  127 us
    pallas_call x1, Pallas kernels, back_one(): pl.pallas_call(functools.partial(back_one_kernel, (rows, cols)), out_shap...  96.3 us
    pallas_call x1, Pallas kernels, gather_first(): pl.pallas_call(functools.partial(first_kernel, sizes, ('xzy', 'zxy', 'yzx...  61.2 us
    unnamed x46, local copies, waits for them, and re-layouts  12.3 us

profile of v3, /device:TPU:0, one launch (start us, length us, event | category | flops | bytes accessed | tf_op | source)
XLA Modules:
  0.0 450.8 jit_solution(14781037475286432641)
XLA Ops:
  1.4 1.4 convert_reduce_fusion.1
  2.8 1.5 multiply_reduce_fusion
  4.3 0.6 broadcast_in_dim.22.refs_2_.refs_0_
  5.5 0.7 dynamic-slice_reduce_fusion
  6.2 0.7 reduce
  6.9 0.6 convert_reduce_fusion
  7.5 0.6 broadcast_in_dim.23.refs_0_
  8.1 1.1 copy.40
  9.2 1.5 convert_bitcast_fusion.1.refs_11_
  10.7 0.7 copy.41
  11.5 0.7 convert_element_type.44.refs_12_
  12.3 0.9 copy.43
  13.2 0.9 copy.44
  14.4 1.3 convert_element_type.37.refs_8_
  15.8 61.2 %gather_first.1 = (bf16[1536,1024]{1,0:T(8,128)(2,1)S(1)}, bf16[1024,1536]{1,0:T(8,128)(2,1)S(1)}, bf16[1024,512]{1,0:T(8,128)(2,1)S(1)}) custom-call(bf16[384,1024]{1,0:T(8,128)(2,1)S(1)} %add_convert_fusion.refs_0_, bf16[3,128,256]{2,1,0:T(8,128)(2,1)S(1)} %convert_element_type.39.refs_1_, bf16[1,128,256]{2,1,0:T(8,128)(2,1)S(1)} %bitcast.41), custom_call_target="tpu_custom_call" | custom-call | tf_op jit(solution)/shard_map/gather_first/pallas_call | solution.py:298
  77.0 2.3 fusion.3.refs_5_.refs_16_
  79.3 0.9 copy-done.2
  80.2 4.8 %convolution_convert_fusion.refs_6_.refs_17_ = bf16[1536,1024]{1,0:T(8,128)(2,1)} fusion(bf16[1536,1024]{1,0:T(8,128)(2,1)S(1)} %get-tuple-element.50.refs_18_, bf16[1024,1536]{1,0:T(8,128)(2,1)S(1)} %get-tuple-element.51.refs_19_), kind=kOutput, calls=%fused_computation.1 | convolution fusion | flops 3222798336 | bytes 8388608 | tf_op jit(solution)/shard_map/dot_general | solution.py:24
  85.0 126.8 %forward.1 = (bf16[1024,512]{1,0:T(8,128)(2,1)}, bf16[1024,1024]{1,0:T(8,128)(2,1)}, bf16[1024,512]{1,0:T(8,128)(2,1)}, bf16[1024,2048]{1,0:T(8,128)(2,1)}, bf16...) custom-call(s32[1,768]{1,0:T(1,128)} %broadcast_in_dim.23.refs_0_, ...), custom_call_target="tpu_custom_call" | custom-call | tf_op jit(solution)/shard_map/forward/pallas_call | solution.py:527
  211.8 96.3 %back_one.1 = (f32[4,128,256]{2,1,0:T(8,128)}, f32[4,128,256]{2,1,0:T(8,128)}, f32[8,1024]{1,0:T(8,128)}, bf16[384,1024]{1,0:T(8,128)(2,1)}, f32[384,1024]{1,0:T...) custom-call(s32[1,768]{1,0:T(1,128)} %broadcast_in_dim.22.refs_2_.refs_0_, ...), custom_call_target="tpu_custom_call" | custom-call | tf_op jit(solution)/shard_map/back_one/pallas_call | solution.py:814
  308.1 130.3 %back_two.1 = (f32[1,128,256]{2,1,0:T(8,128)}, f32[1,128,256]{2,1,0:T(8,128)}, f32[2,128,256]{2,1,0:T(8,128)}, f32[1,128,256]{2,1,0:T(8,128)}, f32[3,128,256]{2,...) custom-call(s32[1,768]{1,0:T(1,128)} %broadcast_in_dim.23.refs_0_, ...), custom_call_target="tpu_custom_call" | custom-call | tf_op jit(solution)/shard_map/back_two/pallas_call | solution.py:1025
  438.4 1.5 slice_bitcast_fusion
  439.9 1.7 copy.47
  441.6 1.7 copy.48
  443.5 1.0 copy.49
  444.5 1.0 copy.46
  445.5 0.9 copy.57
  446.4 1.1 copy.58
  447.5 1.0 copy.59
  448.5 0.7 copy.60
  449.2 0.7 copy.61
  449.9 0.7 copy.62
  (45 shorter events, 1.4 us)
Async XLA Ops:
  0.6 11.5 %copy-start.7 = (f32[128,1024]{1,0:T(8,128)S(1)}, f32[128,1024]{1,0:T(8,128)}, u32[]{:S(2)}) copy-start(f32[128,1024]{1,0:T(8,128)} %param.23) | copy-start | bytes 1572868
  0.7 10.1 %copy-start.15 = (f32[256,128]{1,0:T(8,128)S(1)}, f32[256,128]{1,0:T(8,128)}, u32[]{:S(2)}) copy-start(f32[256,128]{1,0:T(8,128)} %param.22) | copy-start | bytes 393220
  0.7 10.8 %copy-start.13 = (f32[2,128,256]{2,1,0:T(8,128)S(1)}, f32[2,128,256]{2,1,0:T(8,128)}, u32[]{:S(2)}) copy-start(f32[2,128,256]{2,1,0:T(8,128)} %param.21) | copy-start | bytes 786436
  0.7 11.5 %copy-start.11 = (f32[3,128,256]{2,1,0:T(8,128)S(1)}, f32[3,128,256]{2,1,0:T(8,128)}, u32[]{:S(2)}) copy-start(f32[3,128,256]{2,1,0:T(8,128)} %param.18) | copy-start | bytes 1179652
  1.4 11.8 %copy-start.8 = (f32[1024,128]{1,0:T(8,128)S(1)}, f32[1024,128]{1,0:T(8,128)}, u32[]{:S(2)}) copy-start(f32[1024,128]{1,0:T(8,128)} %param.24) | copy-start | bytes 1572868
  8.1 6.0 %copy-start.3 = (bf16[384,1024]{1,0:T(8,128)(2,1)S(1)}, bf16[384,1024]{1,0:T(8,128)(2,1)}, u32[]{:S(2)}) copy-start(bf16[384,1024]{1,0:T(8,128)(2,1)} %refs_20_.1) | copy-start | bytes 2359300
  8.1 6.0 %slice-start = ((f32[3,1024]{1,0:T(4,128)}), f32[1,1024]{1,0:T(1,128)S(1)}, s32[]{:S(2)}) async-start(f32[3,1024]{1,0:T(4,128)} %refs_2_.1), calls=%async_computation | async-start | bytes 8192 | tf_op jit(solution)/shard_map/slice | solution.py:1167
  8.1 6.0 %slice-start.1 = ((f32[3,1024]{1,0:T(4,128)}), f32[1,1024]{1,0:T(1,128)S(1)}, s32[]{:S(2)}) async-start(f32[3,1024]{1,0:T(4,128)} %refs_4_.1), calls=%async_computation.1 | async-start | bytes 8192 | tf_op jit(solution)/shard_map/slice | solution.py:1167
  77.0 2.4 copy-start
  77.0 2.4 copy-start.1
  77.0 3.2 copy-start.2
  308.1 135.2 %copy-start.10 = (f32[4,128,256]{2,1,0:T(8,128)S(1)}, f32[4,128,256]{2,1,0:T(8,128)}, u32[]{:S(2)}) copy-start(f32[4,128,256]{2,1,0:T(8,128)} %get-tuple-element.85) | copy-start | bytes 1572868
  438.4 6.0 %copy-start.9 = (f32[4,128,256]{2,1,0:T(8,128)S(1)}, f32[4,128,256]{2,1,0:T(8,128)}, u32[]{:S(2)}) copy-start(f32[4,128,256]{2,1,0:T(8,128)} %get-tuple-element.86) | copy-start | bytes 1572868
  438.4 7.0 %copy-start.6 = (bf16[384,1024]{1,0:T(8,128)(2,1)S(1)}, bf16[384,1024]{1,0:T(8,128)(2,1)}, u32[]{:S(2)}) copy-start(bf16[384,1024]{1,0:T(8,128)(2,1)} %get-tuple-element.138) | copy-start | bytes 2359300
  443.5 2.9 copy-start.4
  445.5 2.0 copy-start.5
  446.4 2.1 copy-start.12
  447.5 1.7 copy-start.16
  447.5 2.4 copy-start.14
